TPU v7x, 32 devices: a whole 2x2x4 slice. The times are simulated.
32 devices in a mesh: seq: 4 (over y, x), fsdp: 8 (over z, core).
Axes of the slice: x: 2, y: 2, z: 4, core: 2. Of those that a mesh axis runs over, the one named last changes fastest.
Arguments:
- inputs: bfloat16 [8, 512, 3072], P('fsdp', 'seq'), may hold values from -6 to 6
- w_qkv: bfloat16 [3072, 6144], P('fsdp', 'seq'), may hold values from -0.109375 to 0.109375
- saved_qkv: bfloat16 [8, 512, 6144], P('fsdp', 'seq'), may hold values from -60 to 60
- out_grad: bfloat16 [8, 512, 2048], P('fsdp', 'seq'), may hold values from -6 to 6
- clip_grid: int32 [8, 2, 3], P('fsdp'), may hold values from 1 to 2, as said below
- tile_pairs: int32 [8, 4, 6], P('fsdp'), may hold values from -1 to 3, as said below
Outputs:
- input_grad: bfloat16 [8, 512, 3072], P('fsdp', 'seq')
- weight_grad: float32 [3072, 6144], P('fsdp', 'seq')
Inputs may be any that keep to these rules, and one draw needn't show every extreme that they name: `clip_grid`: in each group each clip has 1 x 2 or 2 x 1 tiles a frame (rows times columns is 2), the clips' tiles add up to 4, and group 0's clip 0 has one frame of 1 x 2 tiles. `tile_pairs`: the entries of query tile i, ascending and then -1, are exactly the tiles of i's clip whose frame, row and column tile indices differ from i's by at most one; they lie in tiles 2 * (i // 2 - 1) to 2 * (i // 2 + 2) - 1.
All inputs are finite; a program needn't handle non-finite values.
Results may differ from a plain program's by a relative error of at most 0.012.
The roundings to bfloat16 on the way count: a program that leaves them out, or rounds other values in their place, can miss the bound.
Values may be sent and summed in bfloat16 or wider, within the bound.
A program may use at most 128 MiB of HBM per device.

v0:
```python
import jax
import jax.numpy as jnp
from jax import lax
from jax.sharding import PartitionSpec as P

HD = 128
RT = 16
RH = 56
RW = 56
TT = 2
TH = 8
TW = 8
AREA = 2
TILE = 128


ROPE_BASE = 256.0


def tile_places(layout, tile_count):
    tile_sizes = layout[:, 0] * layout[:, 1] * layout[:, 2]
    clip_ends = jnp.cumsum(tile_sizes, dtype=jnp.int32)
    clip_starts = clip_ends - tile_sizes
    tile_ids = jnp.arange(tile_count, dtype=jnp.int32)
    member = (
        (tile_ids[:, None] >= clip_starts[None, :]) & (tile_ids[:, None] < clip_ends[None, :])
    ).astype(jnp.int32)
    start_of = jnp.sum(member * clip_starts[None, :], axis=1, dtype=jnp.int32)
    rows_of = jnp.sum(member * layout[None, :, 1], axis=1, dtype=jnp.int32)
    cols_of = jnp.sum(member * layout[None, :, 2], axis=1, dtype=jnp.int32)
    local_id = tile_ids - start_of
    within = local_id % (rows_of * cols_of)
    return (local_id // (rows_of * cols_of), within // cols_of, within % cols_of)


def rope_tables(layout, tile_count):
    frame_tile, row_tile, column_tile = tile_places(layout, tile_count)
    inside = jnp.arange(TILE, dtype=jnp.int32)
    frame_pos = (frame_tile[:, None] * TT + (inside // (TH * TW))[None, :]).reshape(-1)
    row_pos = (row_tile[:, None] * TH + (inside // TW % TH)[None, :]).reshape(-1)
    column_pos = (column_tile[:, None] * TW + (inside % TW)[None, :]).reshape(-1)
    angles = []
    for position, section in ((frame_pos, RT), (row_pos, RH), (column_pos, RW)):
        ladder = jnp.arange(section // 2, dtype=jnp.float32) * (2.0 / section)
        frequency = jnp.exp(-jnp.log(jnp.float32(ROPE_BASE)) * ladder)
        spin_angle = position.astype(jnp.float32)[:, None] * frequency[None, :]
        angles += [spin_angle, spin_angle]
    all_angles = jnp.concatenate(angles, axis=1)
    return (jnp.cos(all_angles), jnp.sin(all_angles))


def turn_half(values):
    pieces = []
    offset = 0
    for section in (RT, RH, RW):
        halfway = section // 2
        pieces += [
            -values[..., offset + halfway : offset + section],
            values[..., offset : offset + halfway],
        ]
        offset += section
    return jnp.concatenate(pieces, axis=-1)


def rotate(values, cosine_table, sine_table):
    return values * cosine_table + turn_half(values) * sine_table


def unrotate(values, cosine_table, sine_table):
    return values * cosine_table - turn_half(values * sine_table)


def block_probs(queries, key_block, keep_mask, scale):
    scores = (
        jnp.einsum("nrhd,nchd->nhrc", queries, key_block, preferred_element_type=jnp.float32)
        * scale
    )
    scores = jnp.where(keep_mask[:, None], scores, -jnp.inf)
    highest = jnp.max(scores, axis=-1, keepdims=True)
    expo_terms = jnp.exp(scores - highest)
    return expo_terms / jnp.sum(expo_terms, axis=-1, keepdims=True)


def block_grads(probs_full, queries, key_block, value_block, grad_block, scale):
    probs_low = probs_full.astype(jnp.bfloat16)
    value_grad = jnp.einsum(
        "nhrc,nrhd->nchd", probs_low, grad_block, preferred_element_type=jnp.float32
    )
    prob_grad = jnp.einsum(
        "nrhd,nchd->nhrc", grad_block, value_block, preferred_element_type=jnp.float32
    )
    row_total = jnp.sum(probs_full * prob_grad, axis=-1, keepdims=True)
    score_grad = (probs_full * (prob_grad - row_total) * scale).astype(jnp.bfloat16)
    query_grad = jnp.einsum(
        "nhrc,nchd->nrhd", score_grad, key_block, preferred_element_type=jnp.float32
    )
    key_grad = jnp.einsum(
        "nhrc,nrhd->nchd", score_grad, queries, preferred_element_type=jnp.float32
    )
    return (query_grad, key_grad, value_grad)


def slab_blocks(rot_q, rot_k, values, window):
    tile_count = window.shape[0]
    slab_count = tile_count // AREA
    slab_rows = AREA * TILE
    head_count = rot_q.shape[1]
    queries = rot_q.reshape(slab_count, slab_rows, head_count, HD)

    def band(source):
        padded = jnp.pad(
            source.reshape(slab_count, slab_rows, head_count, HD), ((1, 1), (0, 0), (0, 0), (0, 0))
        )
        return jnp.concatenate(
            [padded[0:slab_count], padded[1 : slab_count + 1], padded[2 : slab_count + 2]], axis=1
        )

    tile_ids = jnp.arange(tile_count, dtype=jnp.int32)
    place = ((tile_ids // AREA - 1) * AREA)[:, None] + jnp.arange(3 * AREA, dtype=jnp.int32)[
        None, :
    ]
    matched = (window[:, :, None] == place[:, None, :]) & (window[:, :, None] >= 0)
    listed = jnp.any(matched, axis=1).reshape(slab_count, AREA, 1, 3 * AREA, 1)
    keep_mask = jnp.broadcast_to(listed, (slab_count, AREA, TILE, 3 * AREA, TILE)).reshape(
        slab_count, slab_rows, 3 * slab_rows
    )
    return (queries, band(rot_k), band(values), keep_mask)


def slab_return(block_grad):
    slab_count = block_grad.shape[0]
    slab_rows = block_grad.shape[1] // 3
    edges = ((0, 0), (0, 0), (0, 0))
    lower = jnp.pad(block_grad[:, :slab_rows], ((0, 2),) + edges)
    middle = jnp.pad(block_grad[:, slab_rows : 2 * slab_rows], ((1, 1),) + edges)
    upper = jnp.pad(block_grad[:, 2 * slab_rows :], ((2, 0),) + edges)
    summed = (lower + middle + upper)[1 : slab_count + 1]
    return summed.reshape(slab_count * slab_rows, block_grad.shape[2], HD)


def body(inputs, w_qkv, saved_qkv, out_grad, clip_grid, tile_pairs):
    window = tile_pairs[0]
    tile_count = window.shape[0]
    scale = HD ** (-0.5)
    group_rows = lax.all_gather(inputs[0], "seq", axis=0, tiled=True)
    head_qkv, head_out = (
        lax.all_to_all(saved_qkv, "seq", split_axis=2, concat_axis=1, tiled=True),
        lax.all_to_all(out_grad, "seq", split_axis=2, concat_axis=1, tiled=True),
    )
    token_count = head_qkv.shape[1]
    head_count = head_qkv.shape[2] // (3 * HD)
    trio_rows = head_qkv[0].reshape(token_count, head_count, 3, HD)
    cosine_table, sine_table = rope_tables(clip_grid[0], tile_count)
    cosine_table = cosine_table[:, None, :]
    sine_table = sine_table[:, None, :]
    rot_q = rotate(trio_rows[:, :, 0].astype(jnp.float32), cosine_table, sine_table).astype(
        jnp.bfloat16
    )
    rot_k = rotate(trio_rows[:, :, 1].astype(jnp.float32), cosine_table, sine_table).astype(
        jnp.bfloat16
    )
    values = trio_rows[:, :, 2]
    queries, key_block, value_block, keep_mask = slab_blocks(rot_q, rot_k, values, window)
    probs_full = block_probs(queries, key_block, keep_mask, scale)
    grad_block = head_out[0].reshape(queries.shape)
    query_grad, key_grad, value_grad = block_grads(
        probs_full, queries, key_block, value_block, grad_block, scale
    )
    query_grad = query_grad.reshape(token_count, head_count, HD)
    key_grad = slab_return(key_grad)
    value_grad = slab_return(value_grad)
    d_query = unrotate(query_grad, cosine_table, sine_table).astype(jnp.bfloat16)
    d_key = unrotate(key_grad, cosine_table, sine_table).astype(jnp.bfloat16)
    d_value = value_grad.astype(jnp.bfloat16)
    qkv_grad = jnp.stack([d_query, d_key, d_value], axis=2).reshape(
        token_count, head_count * 3 * HD
    )
    weight_full = lax.all_gather(w_qkv, "fsdp", axis=0, tiled=True)
    input_part = lax.psum_scatter(
        lax.dot_general(
            qkv_grad, weight_full, (((1,), (1,)), ((), ())), preferred_element_type=jnp.float32
        ).astype(jnp.bfloat16),
        "seq",
        scatter_dimension=0,
        tiled=True,
    )
    weight_part = lax.psum_scatter(
        lax.dot_general(
            group_rows, qkv_grad, (((0,), (0,)), ((), ())), preferred_element_type=jnp.float32
        ).astype(jnp.bfloat16),
        "fsdp",
        scatter_dimension=0,
        tiled=True,
    ).astype(jnp.float32)
    return (input_part[None], weight_part)


def solution(mesh):
    in_specs = (
        P("fsdp", "seq", None),
        P("fsdp", "seq"),
        P("fsdp", "seq", None),
        P("fsdp", "seq", None),
        P("fsdp", None, None),
        P("fsdp", None, None),
    )
    out_specs = (P("fsdp", "seq", None), P("fsdp", "seq"))
    return jax.shard_map(body, mesh=mesh, in_specs=in_specs, out_specs=out_specs, check_vma=False)
```

profile of v0, /device:TPU:8, one launch (start us, length us, event | category | flops | bytes accessed | tf_op | source)
XLA Modules:
  0.0 415.9 jit_solution(12404876076528485043)
XLA Ops:
  8.6 2.4 copy.180
  11.5 11.4 %reduce.7 = bf16[2048,128]{1,0:T(8,128)(2,1)S(1)} reduce(bf16[2048,1,128]{2,1,0:T(2,128)(2,1)S(1)} %bitcast.174, bf16[]{:T(256)} %broadcast.461), dimensions={1}, to_apply=%bitcast.159.reduce_sub_computation | reduce | bytes 1048578
  22.9 0.9 reshape.736
  23.8 4.3 %all-to-all-start.1 = ((bf16[4,2,32768]{2,1,0:T(2,128)(2,1)}), bf16[4,2,32768]{2,1,0:T(2,128)(2,1)}, u32[]{:S(2)}, u32[]{:S(2)}) async-start(bf16[4,2,32768]{2,1,0:T(2,128)(2,1)} %reshape.736), calls=%async_computation.1 | async-start | bytes 1048576 | tf_op jit(solution)/shard_map/all_to_all | solution.py:148
  28.2 6.8 %copy.149 = bf16[1,128,6144]{1,0,2:T(2,128)(2,1)S(1)} copy(bf16[1,128,6144]{2,1,0:T(8,128)(2,1)} %param.8) | data formatting | bytes 3145728 | tf_op args[2]
  35.0 34.3 %reduce.8 = bf16[6144,128]{1,0:T(8,128)(2,1)} reduce(bf16[6144,1,128]{2,1,0:T(2,128)(2,1)S(1)} %bitcast.168, bf16[]{:T(256)} %broadcast.461), dimensions={1}, to_apply=%bitcast.161.reduce_sub_computation | reduce | bytes 3145730
  69.4 3.7 reshape.738
  74.8 1.7 broadcast_in_dim.18
  77.7 4.4 %all-to-all-start = ((bf16[4,2,98304]{2,1,0:T(2,128)(2,1)}), bf16[4,2,98304]{2,1,0:T(2,128)(2,1)}, u32[]{:S(2)}, u32[]{:S(2)}) async-start(bf16[4,2,98304]{2,1,0:T(2,128)(2,1)} %reshape.738), calls=%async_computation | async-start | bytes 3145728 | tf_op jit(solution)/shard_map/all_to_all | solution.py:147
  83.2 1.7 fusion.73
  84.9 1.6 fusion.72
  86.5 2.2 reshape.737
  89.0 0.9 reshape_squeeze.11
  89.9 11.7 %all-to-all-done = bf16[4,2,98304]{2,1,0:T(2,128)(2,1)} async-done(((bf16[4,2,98304]{2,1,0:T(2,128)(2,1)}), bf16[4,2,98304]{2,1,0:T(2,128)(2,1)}, u32[]{:S(2)}, u32[]{:S(2)}) %all-to-all-start) | async-done | bytes 1572896 | tf_op jit(solution)/shard_map/all_to_all | solution.py:147
  101.7 3.1 reshape.739
  104.9 7.3 %copy.150 = bf16[1,4,128,1536]{2,1,3,0:T(4,128)(2,1)S(1)} copy(bf16[1,4,128,1536]{2,3,1,0:T(8,128)(2,1)S(1)} %bitcast.170) | data formatting | bytes 3145728 | tf_op jit(solution)/shard_map/all_to_all | solution.py:147
  112.3 1.1 reshape_squeeze.9
  113.4 2.1 fusion.67
  115.5 2.6 copy.151
  118.1 1.6 fusion.69
  120.1 0.9 concatenate.99
  121.0 1.3 copy.158
  122.3 1.3 fusion.68
  123.6 1.2 reshape.722
  125.2 1.1 reshape.723
  126.3 1.3 copy.160
  127.8 1.4 copy.161
  129.3 1.4 copy.162
  130.7 1.3 copy.171
  132.0 1.3 copy.172
  133.5 1.4 copy.173
  134.9 0.8 reshape.727
  135.7 2.4 copy.174
  138.1 1.8 reshape.728
  139.9 2.3 copy.175
  142.2 1.8 reshape.729
  144.0 2.3 copy.176
  146.3 2.6 copy.165
  148.9 4.5 %concatenate.104 = f32[2,256,4,128]{3,1,2,0:T(8,128)} concatenate(f32[2,256,4,8]{3,1,2,0:T(8,128)S(1)} %copy.157, f32[2,256,4,8]{3,1,2,0:T(8,128)S(1)} %copy-done.1, f32[2,256,4,28]{3,1,2,0:T(8,128)S(1)} %copy.159, f32[2,256,4,28]{3,1,2,0:T(8,128)} %copy.160, f32[2,256,4,28]{3,1,2,0:T(8,128)} %copy.161, f32[2,256,4,28]{3,1,2,0:T(8,128)} %copy.162), dimensions={3} | concatenate | bytes 2097152 | tf_op jit(solution)/shard_map/concatenate | solution.py:62
  153.4 4.3 %concatenate.112 = f32[2,256,4,128]{3,1,2,0:T(8,128)S(1)} concatenate(f32[2,256,4,8]{3,1,2,0:T(8,128)} %copy.171, f32[2,256,4,8]{3,1,2,0:T(8,128)} %copy.172, f32[2,256,4,28]{3,1,2,0:T(8,128)} %copy.173, f32[2,256,4,28]{3,1,2,0:T(8,128)} %copy.174, f32[2,256,4,28]{3,1,2,0:T(8,128)} %copy.175, f32[2,256,4,28]{3,1,2,0:T(8,128)} %copy.176), dimensions={3} | concatenate | bytes 2097152 | tf_op jit(solution)/shard_map/concatenate | solution.py:62
  157.7 1.8 fusion.41
  159.7 1.0 fusion.42
  160.8 2.8 fusion.74
  163.6 1.9 fusion.17
  166.5 0.8 copy.192
  167.8 3.6 fusion.20
  171.5 21.5 %fusion.26 = f32[2,256,4,128]{1,3,2,0:T(8,128)} fusion(f32[2,4,768,256]{2,3,1,0:T(8,128)} %fusion.20, bf16[2,256,4,128]{3,1,2,0:T(8,128)(2,1)S(1)} %get-tuple-element.58, bf16[2,256,4,128]{3,1,2,0:T(8,128)(2,1)S(1)} %get-tuple-element.59, bf16[2,256,4,128]{3,1,2,0:T(8,128)(2,1)S(1)} %get-tuple-element.57, f32[2,4,256,768]{3,2,1,0:T(8,128)} %copy-done.20, ...), kind=kOutput, calls=%fused_computation.33 | convolution fusion | flops 418384640 | bytes 15212544 | tf_op jit(solution)/shard_map/nhrc,nchd->nrhd/dot_general | solution.py:94
  192.9 1.5 copy.185
  194.5 21.5 %fusion.16 = f32[2,768,4,128]{1,3,2,0:T(8,128)} fusion(bf16[2,256,4,128]{3,1,2,0:T(8,128)(2,1)S(1)} %copy-done.8, f32[2,4,768,256]{2,3,1,0:T(8,128)} %fusion.20, f32[2,4,256,768]{3,2,1,0:T(8,128)} %copy-done.20, f32[2,4,256]{2,1,0:T(4,128)S(1)} %get-tuple-element.75), kind=kOutput, calls=%fused_computation.23 | convolution fusion | flops 413666048 | bytes 16261120 | tf_op jit(solution)/shard_map/nhrc,nrhd->nchd/dot_general | solution.py:97
  216.0 2.2 fusion.65
  218.9 1.7 slice_bitcast_fusion.5
  220.5 3.1 slice_bitcast_fusion.3
  223.7 5.0 %concatenate.121 = f32[512,4,1,128]{3,0,1,2:T(8,128)} concatenate(f32[512,4,1,8]{3,0,1,2:T(8,128)} %get-tuple-element.36, f32[512,4,1,8]{3,0,1,2:T(8,128)} %get-tuple-element.35, f32[512,4,1,28]{3,0,1,2:T(8,128)} %get-tuple-element.34, f32[512,4,1,28]{3,0,1,2:T(8,128)} %get-tuple-element.33, f32[512,4,1,28]{3,0,1,2:T(8,128)} %get-tuple-element.32, ...), dimensions={3} | concatenate | bytes 2097152 | tf_op jit(solution)/shard_map/concatenate | solution.py:62
  228.7 1.7 slice_bitcast_fusion.2
  230.4 3.1 slice_bitcast_fusion
  233.5 5.2 %concatenate.128 = f32[512,4,1,128]{3,0,1,2:T(8,128)} concatenate(f32[512,4,1,8]{3,0,1,2:T(8,128)} %get-tuple-element.42, f32[512,4,1,8]{3,0,1,2:T(8,128)} %get-tuple-element.41, f32[512,4,1,28]{3,0,1,2:T(8,128)} %get-tuple-element.40, f32[512,4,1,28]{3,0,1,2:T(8,128)} %get-tuple-element.39, f32[512,4,1,28]{3,0,1,2:T(8,128)} %get-tuple-element.38, ...), dimensions={3} | concatenate | bytes 2097152 | tf_op jit(solution)/shard_map/concatenate | solution.py:62
  238.7 1.6 fusion.37
  241.2 9.6 %fusion.2 = bf16[3072,1536]{0,1:T(8,128)(2,1)} fusion(bf16[512,1536]{0,1:T(8,128)(2,1)S(1)} %bitcast.179, bf16[1,512,3072]{2,1,0:T(8,128)(2,1)} %all-gather.6.cloned.1.call-done), kind=kOutput, calls=%fused_computation.3 | convolution fusion | flops 4836556800 | bytes 14155776 | tf_op jit(solution)/shard_map/dot_general | solution.py:188
  250.8 12.7 %copy.215 = bf16[3072,1536]{1,0:T(8,128)(2,1)} copy(bf16[3072,1536]{0,1:T(8,128)(2,1)} %fusion.2) | data formatting | bytes 18874368
  263.5 10.2 %convolution_convert_fusion.1 = bf16[512,3072]{1,0:T(8,128)(2,1)} fusion(bf16[512,1536]{0,1:T(8,128)(2,1)S(1)} %bitcast.180, bf16[3072,1536]{1,0:T(8,128)(2,1)} %all-gather.4.cloned.1.call-done), kind=kOutput, calls=%fused_computation.12 | convolution fusion | flops 4833411072 | bytes 14155776 | tf_op jit(solution)/shard_map/dot_general | solution.py:180
  273.8 86.7 %reduce-scatter.7.cloned.1.call-done = bf16[384,1536]{1,0:T(8,128)(2,1)} async-done(((bf16[3072,1536]{1,0:T(8,128)(2,1)}), bf16[384,1536]{1,0:T(8,128)(2,1)}) %reduce-scatter.7.cloned.1.call-update) | async-done | bytes 1179664
  360.5 1.7 copy.216
  362.2 1.8 copy.194
  364.0 45.1 %reduce-scatter.5.cloned.1.call-done = bf16[128,3072]{1,0:T(8,128)(2,1)} async-done(((bf16[512,3072]{1,0:T(8,128)(2,1)}), bf16[128,3072]{1,0:T(8,128)(2,1)}) %reduce-scatter.5.cloned.1.call-update) | async-done | bytes 786448 | tf_op jit(solution)/shard_map/reduce_scatter | solution.py:179
  (114 shorter events, 11.0 us)
Async XLA Ops:
  7.2 234.0 %all-gather.6.cloned.1.call-start = ((), (), s32[]{:S(2)}) async-start(), calls=%async_computation.6 | async-start | bytes 3932160 | tf_op jit(solution)/shard_map/all_gather | solution.py:145
  7.9 255.6 %all-gather.4.cloned.1.call-start = ((), (), s32[]{:S(2)}) async-start(), calls=%async_computation.4 | async-start | bytes 10616832 | tf_op jit(solution)/shard_map/all_gather | solution.py:178
  23.8 53.8 %all-to-all-start.1 = ((bf16[4,2,32768]{2,1,0:T(2,128)(2,1)}), bf16[4,2,32768]{2,1,0:T(2,128)(2,1)}, u32[]{:S(2)}, u32[]{:S(2)}) async-start(bf16[4,2,32768]{2,1,0:T(2,128)(2,1)} %reshape.736), calls=%async_computation.1 | async-start | bytes 1048576 | tf_op jit(solution)/shard_map/all_to_all | solution.py:148
  35.0 38.1 %copy-start.18 = (s32[1,2,3]{2,1,0:T(2,128)S(1)}, s32[1,2,3]{2,1,0:T(2,128)}, u32[]{:S(2)}) copy-start(s32[1,2,3]{2,1,0:T(2,128)} %param.10) | copy-start | bytes 76
  35.0 39.2 %copy-start.19 = (s32[1,4,6]{2,1,0:T(4,128)S(1)}, s32[1,4,6]{2,1,0:T(4,128)}, u32[]{:S(2)}) copy-start(s32[1,4,6]{2,1,0:T(4,128)} %param.11) | copy-start | bytes 292
  77.7 24.0 %all-to-all-start = ((bf16[4,2,98304]{2,1,0:T(2,128)(2,1)}), bf16[4,2,98304]{2,1,0:T(2,128)(2,1)}, u32[]{:S(2)}, u32[]{:S(2)}) async-start(bf16[4,2,98304]{2,1,0:T(2,128)(2,1)} %reshape.738), calls=%async_computation | async-start | bytes 3145728 | tf_op jit(solution)/shard_map/all_to_all | solution.py:147
  82.1 278.4 %reduce-scatter.7.cloned.1.call-start = ((), (), s32[]{:S(2)}) async-start(), calls=%async_computation.7 | async-start | bytes 10616832
  115.5 6.8 %copy-start = (f32[512,4,128]{0,2,1:T(8,128)S(1)}, f32[512,4,128]{0,2,1:T(8,128)}, u32[]{:S(2)}) copy-start(f32[512,4,128]{0,2,1:T(8,128)} %get-tuple-element.28) | copy-start | bytes 3145732
  123.6 4.0 copy-start.14
  123.6 5.5 %copy-start.13 = (f32[512,4,28]{0,2,1:T(8,128)S(1)}, f32[512,4,28]{0,2,1:T(8,128)}, u32[]{:S(2)}) copy-start(f32[512,4,28]{0,2,1:T(8,128)} %get-tuple-element.43) | copy-start | bytes 688132
  124.8 5.8 %copy-start.17 = (f32[512,4,8]{0,2,1:T(8,128)S(1)}, f32[512,4,8]{0,2,1:T(8,128)}, u32[]{:S(2)}) copy-start(f32[512,4,8]{0,2,1:T(8,128)} %get-tuple-element.85) | copy-start | bytes 196612
  127.6 5.8 %copy-start.12 = (f32[512,4,28]{0,2,1:T(8,128)S(1)}, f32[512,4,28]{0,2,1:T(8,128)}, u32[]{:S(2)}) copy-start(f32[512,4,28]{0,2,1:T(8,128)} %get-tuple-element.81) | copy-start | bytes 688132
  129.1 5.8 %copy-start.11 = (f32[512,4,28]{0,2,1:T(8,128)S(1)}, f32[512,4,28]{0,2,1:T(8,128)}, u32[]{:S(2)}) copy-start(f32[512,4,28]{0,2,1:T(8,128)} %get-tuple-element.82) | copy-start | bytes 688132
  135.7 13.2 %copy-start.1 = (f32[2,256,4,8]{3,1,2,0:T(8,128)S(1)}, f32[2,256,4,8]{3,1,2,0:T(8,128)}, u32[]{:S(2)}) copy-start(f32[2,256,4,8]{3,1,2,0:T(8,128)} %copy.158) | copy-start | bytes 196612
  153.4 4.3 %copy-start.3 = (f32[2,256,4,128]{3,1,2,0:T(8,128)S(1)}, f32[2,256,4,128]{3,1,2,0:T(8,128)}, u32[]{:S(2)}) copy-start(f32[2,256,4,128]{3,1,2,0:T(8,128)} %concatenate.104) | copy-start | bytes 3145732
  153.4 4.3 %copy-start.9 = (f32[2,256,128]{2,1,0:T(8,128)S(1)}, f32[2,256,128]{2,1,0:T(8,128)}, u32[]{:S(2)}) copy-start(f32[2,256,128]{2,1,0:T(8,128)} %get-tuple-element.67) | copy-start | bytes 786436
  153.4 4.3 %copy-start.10 = (f32[2,256,128]{2,1,0:T(8,128)S(1)}, f32[2,256,128]{2,1,0:T(8,128)}, u32[]{:S(2)}) copy-start(f32[2,256,128]{2,1,0:T(8,128)} %get-tuple-element.68) | copy-start | bytes 786436
  159.6 1.1 copy-start.7
  159.7 1.1 copy-start.16
  160.8 2.8 copy-start.4
  163.6 2.6 copy-start.20
  166.4 1.0 copy-start.5
  171.5 23.0 %copy-start.8 = (bf16[2,256,4,128]{3,1,2,0:T(8,128)(2,1)S(1)}, bf16[2,256,4,128]{3,1,2,0:T(8,128)(2,1)}, u32[]{:S(2)}) copy-start(bf16[2,256,4,128]{3,1,2,0:T(8,128)(2,1)} %copy-done.7) | copy-start | bytes 1572868
  233.5 5.2 %copy-start.2 = (f32[512,4,1,128]{3,0,1,2:T(8,128)S(1)}, f32[512,4,1,128]{3,0,1,2:T(8,128)}, u32[]{:S(2)}) copy-start(f32[512,4,1,128]{3,0,1,2:T(8,128)} %concatenate.121) | copy-start | bytes 3145732
  233.5 5.2 %copy-start.15 = (f32[512,128]{1,0:T(8,128)S(1)}, f32[512,128]{1,0:T(8,128)}, u32[]{:S(2)}) copy-start(f32[512,128]{1,0:T(8,128)} %get-tuple-element.65) | copy-start | bytes 786436
  238.6 1.6 copy-start.6
  263.5 145.6 %reduce-scatter.5.cloned.1.call-start = ((), (), s32[]{:S(2)}) async-start(), calls=%async_computation.5 | async-start | bytes 3932160 | tf_op jit(solution)/shard_map/reduce_scatter | solution.py:179
Sparse Core Ops, SparseCore 0:
  9.8 45.1 all-gather.5
  56.7 87.9 all-gather.3
  263.6 96.8 reduce-scatter.6
  363.9 45.1 reduce-scatter.4
where the time goes:
time: 424 us; the launch traced here: 416 us
  waiting for transfers between devices  145 us (34%)
  local copies, waits for them, and re-layouts  109 us (26%)
  matrix products  69.3 us (16%)
  other arithmetic  69 us (16%)
  between operations  14.6 us (3%)
  starting transfers between devices  9.13 us (2%)
    unnamed x5, waiting for transfers between devices  88.1 us
    unnamed x2, other arithmetic  45.8 us
    reduce_scatter x1, waiting for transfers between devices, body(): lax.psum_scatter(lax.dot_general(qkv_grad, weight_full, (((1,), (1,)), ((...  45.1 us
    concatenate x28, local copies, waits for them, and re-layouts, turn_half(): return jnp.concatenate(pieces, axis=-1)  44.2 us
    unnamed x57, local copies, waits for them, and re-layouts  37.1 us
    dot_general x1, matrix products, block_grads(): jnp.einsum('nhrc,nrhd->nchd', score_grad, queries, preferred_element_type...  21.5 us
    dot_general x1, matrix products, block_grads(): jnp.einsum('nhrc,nchd->nrhd', score_grad, key_block, preferred_element_ty...  21.5 us
    all_to_all x1, waiting for transfers between devices, body(): lax.all_to_all(saved_qkv, 'seq', split_axis=2, concat_axis=1, tiled=True)  11.7 us
  transfers between devices with their start and end apart: 6, of which 3 were waited for; matrix products, arithmetic and copies ran while one was open for 59% of the time, Pallas kernels for 0%

commit v1 on v0

v1 whole, which is shorter than its diff:
```python
import functools

import jax
import jax.numpy as jnp
from jax import lax
from jax.experimental import pallas as pl
from jax.experimental.pallas import tpu as pltpu
from jax.sharding import PartitionSpec as P

HD = 128
RT = 16
RH = 56
RW = 56
TT = 2
TH = 8
TW = 8
AREA = 2
TILE = 128


ROPE_BASE = 256.0


def tile_places(layout, tile_count):
    tile_sizes = layout[:, 0] * layout[:, 1] * layout[:, 2]
    clip_ends = jnp.cumsum(tile_sizes, dtype=jnp.int32)
    clip_starts = clip_ends - tile_sizes
    tile_ids = jnp.arange(tile_count, dtype=jnp.int32)
    member = (
        (tile_ids[:, None] >= clip_starts[None, :]) & (tile_ids[:, None] < clip_ends[None, :])
    ).astype(jnp.int32)
    start_of = jnp.sum(member * clip_starts[None, :], axis=1, dtype=jnp.int32)
    rows_of = jnp.sum(member * layout[None, :, 1], axis=1, dtype=jnp.int32)
    cols_of = jnp.sum(member * layout[None, :, 2], axis=1, dtype=jnp.int32)
    local_id = tile_ids - start_of
    within = local_id % (rows_of * cols_of)
    return (local_id // (rows_of * cols_of), within // cols_of, within % cols_of)


def rope_tables(layout, tile_count):
    frame_tile, row_tile, column_tile = tile_places(layout, tile_count)
    inside = jnp.arange(TILE, dtype=jnp.int32)
    frame_pos = (frame_tile[:, None] * TT + (inside // (TH * TW))[None, :]).reshape(-1)
    row_pos = (row_tile[:, None] * TH + (inside // TW % TH)[None, :]).reshape(-1)
    column_pos = (column_tile[:, None] * TW + (inside % TW)[None, :]).reshape(-1)
    angles = []
    for position, section in ((frame_pos, RT), (row_pos, RH), (column_pos, RW)):
        ladder = jnp.arange(section // 2, dtype=jnp.float32) * (2.0 / section)
        frequency = jnp.exp(-jnp.log(jnp.float32(ROPE_BASE)) * ladder)
        spin_angle = position.astype(jnp.float32)[:, None] * frequency[None, :]
        angles += [spin_angle, spin_angle]
    all_angles = jnp.concatenate(angles, axis=1)
    signs = []
    for section in (RT, RH, RW):
        signs += [-jnp.ones((section // 2,), jnp.float32), jnp.ones((section // 2,), jnp.float32)]
    return (jnp.cos(all_angles), jnp.sin(all_angles) * jnp.concatenate(signs)[None, :])


def partner(values):
    lane = lax.broadcasted_iota(jnp.int32, values.shape, 1)
    short, long = RT // 2, RH // 2
    first = (lane < RT + long) | ((lane >= RT + RH) & (lane < RT + RH + long))
    wide = jnp.where(
        first, pltpu.roll(values, HD - long, 1), pltpu.roll(values, long, 1)
    )
    narrow = jnp.where(
        lane < short, pltpu.roll(values, HD - short, 1), pltpu.roll(values, short, 1)
    )
    return jnp.where(lane < RT, narrow, wide)


def attention_kernel(qkv_ref, grad_ref, cos_ref, sin_ref, bias_ref, out_ref, dk_ref, dv_ref):
    rows = AREA * TILE
    slabs = qkv_ref.shape[0] // rows
    scale = HD ** (-0.5)
    cosine, sine = cos_ref[...], sin_ref[...]

    def rotated(start):
        values = qkv_ref[:, start : start + HD].astype(jnp.float32)
        return (values * cosine + partner(values) * sine).astype(jnp.bfloat16)

    rot_q, rot_k = rotated(0), rotated(HD)
    values = qkv_ref[:, 2 * HD : 3 * HD]
    grads = grad_ref[...]
    across = (((1,), (1,)), ((), ()))
    plain = (((1,), (0,)), ((), ()))
    down = (((0,), (0,)), ((), ()))
    dk_ref[...] = jnp.zeros_like(dk_ref)
    dv_ref[...] = jnp.zeros_like(dv_ref)
    for slab in range(slabs):
        here = slice(slab * rows, (slab + 1) * rows)
        near = slice(max(0, slab - 1) * rows, min(slabs, slab + 2) * rows)
        width = near.stop - near.start
        query, grad, key, value = rot_q[here], grads[here], rot_k[near], values[near]
        bias = jnp.concatenate(
            [
                jnp.broadcast_to(bias_ref[tile : tile + 1, near], (TILE, width))
                for tile in range(slab * AREA, (slab + 1) * AREA)
            ],
            axis=0,
        )
        scores = lax.dot_general(query, key, across, preferred_element_type=jnp.float32)
        scores = scores * scale + bias
        expo = jnp.exp(scores - jnp.max(scores, axis=-1, keepdims=True))
        probs = expo * (1.0 / jnp.sum(expo, axis=-1, keepdims=True))
        dv_ref[near, :] += lax.dot_general(
            probs.astype(jnp.bfloat16), grad, down, preferred_element_type=jnp.float32
        )
        prob_grad = lax.dot_general(grad, value, across, preferred_element_type=jnp.float32)
        total = jnp.sum(probs * prob_grad, axis=-1, keepdims=True)
        score_grad = (probs * (prob_grad - total) * scale).astype(jnp.bfloat16)
        dq = lax.dot_general(score_grad, key, plain, preferred_element_type=jnp.float32)
        dq = dq * cosine[here] - partner(dq) * sine[here]
        out_ref[here, 0:HD] = dq.astype(jnp.bfloat16)
        dk_ref[near, :] += lax.dot_general(
            score_grad, query, down, preferred_element_type=jnp.float32
        )
    dk = dk_ref[...]
    out_ref[:, HD : 2 * HD] = (dk * cosine - partner(dk) * sine).astype(jnp.bfloat16)
    out_ref[:, 2 * HD : 3 * HD] = dv_ref[...].astype(jnp.bfloat16)


def attention(mixed, cosine, sine, bias):
    tokens = mixed.shape[0]
    heads = mixed.shape[1] // (4 * HD)
    whole = lambda array: pl.BlockSpec(array.shape, lambda head: (0, 0))
    return pl.pallas_call(
        attention_kernel,
        grid=(heads,),
        out_shape=jax.ShapeDtypeStruct((tokens, heads * 3 * HD), jnp.bfloat16),
        in_specs=[
            pl.BlockSpec((tokens, 3 * HD), lambda head: (0, head)),
            pl.BlockSpec((tokens, HD), lambda head: (0, 3 * heads + head)),
            whole(cosine),
            whole(sine),
            whole(bias),
        ],
        out_specs=pl.BlockSpec((tokens, 3 * HD), lambda head: (0, head)),
        scratch_shapes=[
            pltpu.VMEM((tokens, HD), jnp.float32),
            pltpu.VMEM((tokens, HD), jnp.float32),
        ],
        compiler_params=pltpu.CompilerParams(vmem_limit_bytes=48 * 1024 * 1024),
        cost_estimate=pl.CostEstimate(
            flops=heads * 10 * tokens * min(tokens, 768) * HD,
            bytes_accessed=16 * heads * tokens * HD,
            transcendentals=heads * tokens * min(tokens, 768),
        ),
    )(mixed, mixed, cosine, sine, bias)


def by_device(rows, parts):
    tokens, columns = rows.shape
    return rows.reshape(tokens, parts, columns // parts).transpose(1, 0, 2)


def body(seq_size, fsdp_size, inputs, w_qkv, saved_qkv, out_grad, clip_grid, tile_pairs):
    window = tile_pairs[0]
    tile_count = window.shape[0]
    mixed = jnp.concatenate(
        [by_device(saved_qkv[0], seq_size), by_device(out_grad[0], seq_size)], axis=2
    )
    mixed = lax.all_to_all(mixed, "seq", split_axis=0, concat_axis=0, tiled=True)
    mixed = mixed.reshape(-1, mixed.shape[2])
    weight_full = lax.all_gather(w_qkv, "fsdp", axis=0, tiled=True)
    group_rows = lax.all_gather(inputs[0], "seq", axis=0, tiled=True)
    cosine, sine = rope_tables(clip_grid[0], tile_count)
    listed = jnp.any(
        window[:, :, None] == jnp.arange(tile_count, dtype=jnp.int32)[None, None, :], axis=1
    )
    bias = jnp.repeat(jnp.where(listed, 0.0, -1e30).astype(jnp.float32), TILE, axis=1)
    qkv_grad = attention(mixed, cosine, sine, bias)
    weight_part = lax.psum_scatter(
        lax.dot_general(
            group_rows, qkv_grad, (((0,), (0,)), ((), ())), preferred_element_type=jnp.float32
        ).astype(jnp.bfloat16),
        "fsdp",
        scatter_dimension=0,
        tiled=True,
    ).astype(jnp.float32)
    input_part = lax.psum_scatter(
        lax.dot_general(
            qkv_grad, weight_full, (((1,), (1,)), ((), ())), preferred_element_type=jnp.float32
        ).astype(jnp.bfloat16),
        "seq",
        scatter_dimension=0,
        tiled=True,
    )
    return (input_part[None], weight_part)


def solution(mesh):
    in_specs = (
        P("fsdp", "seq", None),
        P("fsdp", "seq"),
        P("fsdp", "seq", None),
        P("fsdp", "seq", None),
        P("fsdp", None, None),
        P("fsdp", None, None),
    )
    out_specs = (P("fsdp", "seq", None), P("fsdp", "seq"))
    local = functools.partial(body, mesh.shape["seq"], mesh.shape["fsdp"])
    return jax.shard_map(local, mesh=mesh, in_specs=in_specs, out_specs=out_specs, check_vma=False)
```

time: 424 us -> 321 us (0.76); the launches traced: 416 us -> 319 us
  waiting for transfers between devices: 145 us -> 242 us
  local copies, waits for them, and re-layouts: 109 us -> 23.4 us
  other arithmetic: 69 us -> 4.02 us
  matrix products: 69.3 us -> 19.8 us
  Pallas kernels: 0 us -> 11 us
  starting transfers between devices: 9.13 us -> 4.15 us
    all_gather x1, waiting for transfers between devices: 0.02 us -> 66.8 us  [body(): weight_full = lax.all_gather(w_qkv, 'fsdp', axis=0, tiled=True)]
    dot_general x5 -> x0, matrix products: 49.5 us -> none  [the longest x1 21.5 us: block_grads(): jnp.einsum('nhrc,nrhd->nchd', score_grad, queries, preferred_element_type...]
    unnamed x2 -> x0, other arithmetic: 45.8 us -> none
    concatenate x28 -> x0, local copies, waits for them, and re-layouts: 44.2 us -> none  [turn_half(): return jnp.concatenate(pieces, axis=-1)]
    unnamed x57 -> x15, local copies, waits for them, and re-layouts: 37.1 us -> 17.6 us
    all_to_all x2 -> x1, waiting for transfers between devices: 11.7 us -> 30.1 us  [body(): lax.all_to_all(mixed, 'seq', split_axis=0, concat_axis=0, tiled=True)]
    pallas_call x0 -> x1, Pallas kernels: none -> 11 us  [attention(): pl.pallas_call(attention_kernel, grid=(heads,), out_shape=jax.ShapeDtypeS...]
    all_gather x1, waiting for transfers between devices: 0.02 us -> 8.74 us  [body(): group_rows = lax.all_gather(inputs[0], 'seq', axis=0, tiled=True)]
  transfers between devices with their start and end apart: 6 -> 5, of which waited for: 3 -> 5; matrix products, arithmetic and copies ran while one was open for 59% -> 14% of each run, Pallas kernels for 0% -> 3%
where the time goes in v1:
time: 321 us; the launch traced here: 319 us
  waiting for transfers between devices  242 us (75%)
  local copies, waits for them, and re-layouts  23.4 us (7%)
  matrix products  19.8 us (6%)
  between operations  13.9 us (4%)
  Pallas kernels  11 us (3%)
  starting transfers between devices  4.15 us (1%)
  other arithmetic  4.02 us (1%)
    unnamed x5, waiting for transfers between devices  91.5 us
    all_gather x1, waiting for transfers between devices, body(): weight_full = lax.all_gather(w_qkv, 'fsdp', axis=0, tiled=True)  66.8 us
    reduce_scatter x1, waiting for transfers between devices, body(): lax.psum_scatter(lax.dot_general(qkv_grad, weight_full, (((1,), (1,)), ((...  45.1 us
    all_to_all x1, waiting for transfers between devices, body(): lax.all_to_all(mixed, 'seq', split_axis=0, concat_axis=0, tiled=True)  30.1 us
    unnamed x15, local copies, waits for them, and re-layouts  17.6 us
    pallas_call x1, Pallas kernels, attention(): pl.pallas_call(attention_kernel, grid=(heads,), out_shape=jax.ShapeDtypeS...  11 us
    dot_general x1, matrix products, body(): lax.dot_general(qkv_grad, weight_full, (((1,), (1,)), ((), ())), preferre...  10.1 us
    dot_general x1, matrix products, body(): lax.dot_general(group_rows, qkv_grad, (((0,), (0,)), ((), ())), preferred...  9.67 us
  transfers between devices with their start and end apart: 5, of which 5 were waited for; matrix products, arithmetic and copies ran while one was open for 14% of the time, Pallas kernels for 3%

profile of v1, /device:TPU:8, one launch (start us, length us, event | category | flops | bytes accessed | tf_op | source)
XLA Modules:
  0.0 318.6 jit_solution(15007776315121208298)
XLA Ops:
  7.2 0.0 all-gather.6.cloned.1.call-start
  7.2 0.7 all-gather.6.cloned.1.call-update
  7.9 0.0 all-gather.4.cloned.1.call-start
  7.9 0.7 all-gather.4.cloned.1.call-update
  8.6 1.4 reshape_squeeze.7
  10.1 0.1 copy.27
  10.2 3.6 %reshape_squeeze.6 = bf16[128,4,1536]{2,1,0:T(4,128)(2,1)S(1)} reshape(bf16[1,128,6144]{2,1,0:T(8,128)(2,1)} %param.8) | data formatting | bytes 3145728 | tf_op jit(solution)/shard_map/reshape;squeeze | solution.py:154
  13.8 0.3 copy.26
  14.1 1.6 pad_maximum_fusion
  15.7 0.0 copy-start.2
  15.7 0.0 copy-start.3
  15.7 3.8 %all-to-all-start = ((bf16[4,128,2048]{2,1,0:T(8,128)(2,1)}), bf16[4,128,2048]{2,1,0:T(8,128)(2,1)S(1)}, u32[]{:S(2)}, u32[]{:S(2)}) async-start(bf16[4,128,2048]{2,1,0:T(8,128)(2,1)} %pad_maximum_fusion), calls=%async_computation | async-start | bytes 4194304 | tf_op jit(solution)/shard_map/all_to_all | solution.py:163
  19.5 0.0 copy-start.4
  19.5 0.0 reduce-scatter.7.cloned.1.call-start
  19.5 0.0 copy-done.2
  19.5 0.2 slice_reduce_fusion.1
  19.8 0.1 reduce
  19.9 0.0 copy-done.3
  19.9 0.1 fusion.2
  20.1 0.1 broadcast_bitcast_fusion
  20.2 0.1 select_reduce_fusion
  20.3 0.3 fusion.6
  20.6 0.1 fusion.5
  20.7 0.1 convert_bitcast_fusion.1
  20.8 0.1 convert_bitcast_fusion
  20.8 0.1 broadcast_multiply_fusion.2
  21.0 0.2 broadcast_multiply_fusion
  21.2 0.4 concatenate.7
  21.6 0.0 copy-done.4
  21.6 0.9 sine_multiply_fusion
  22.6 30.1 %all-to-all-done = bf16[4,128,2048]{2,1,0:T(8,128)(2,1)S(1)} async-done(((bf16[4,128,2048]{2,1,0:T(8,128)(2,1)}), bf16[4,128,2048]{2,1,0:T(8,128)(2,1)S(1)}, u32[]{:S(2)}, u32[]{:S(2)}) %all-to-all-start) | async-done | bytes 2097184 | tf_op jit(solution)/shard_map/all_to_all | solution.py:163
  52.7 11.0 %shard_map.77 = bf16[512,1536]{1,0:T(8,128)(2,1)S(1)} custom-call(bf16[512,2048]{1,0:T(8,128)(2,1)S(1)} %bitcast.30, bf16[512,2048]{1,0:T(8,128)(2,1)S(1)} %bitcast.31, f32[512,128]{1,0:T(8,128)S(1)} %get-tuple-element.19.cos_ref, f32[512,128]{1,0:T(8,128)S(1)} %get-tuple-element.18.sin_ref, f32[4,512]{1,0:T(4,128)S(1)} %bitcast.32), custom_call_target="tpu_custom_call" | custom-call | flops 1342177280 | bytes 4194304 | tf_op jit(solution)/shard_map/pallas_call | solution.py:127
  63.7 0.0 copy-start
  63.7 1.1 copy-done
  64.8 8.7 %all-gather.6.cloned.1.call-done = bf16[1,512,3072]{2,1,0:T(8,128)(2,1)} async-done(((bf16[1,128,3072]{2,1,0:T(8,128)(2,1)}), bf16[1,512,3072]{2,1,0:T(8,128)(2,1)}) %all-gather.6.cloned.1.call-update) | async-done | bytes 3145744 | tf_op jit(solution)/shard_map/all_gather | solution.py:166
  73.6 9.7 %fusion = bf16[3072,1536]{0,1:T(8,128)(2,1)} fusion(bf16[512,1536]{1,0:T(8,128)(2,1)} %copy-done, bf16[1,512,3072]{2,1,0:T(8,128)(2,1)} %all-gather.6.cloned.1.call-done), kind=kOutput, calls=%fused_computation.1 | convolution fusion | flops 4836556800 | bytes 14155776 | tf_op jit(solution)/shard_map/dot_general | solution.py:174
  83.2 12.9 %copy.20 = bf16[3072,1536]{1,0:T(8,128)(2,1)} copy(bf16[3072,1536]{0,1:T(8,128)(2,1)} %fusion) | data formatting | bytes 18874368
  96.1 0.0 copy-start.1
  96.1 0.0 reduce-scatter.7.cloned.1.call-update
  96.2 0.2 reduce-scatter.5.cloned.1.call-start
  96.4 66.8 %all-gather.4.cloned.1.call-done = bf16[3072,1536]{1,0:T(8,128)(2,1)} async-done(((bf16[384,1536]{1,0:T(8,128)(2,1)}), bf16[3072,1536]{1,0:T(8,128)(2,1)}) %all-gather.4.cloned.1.call-update) | async-done | bytes 9437200 | tf_op jit(solution)/shard_map/all_gather | solution.py:165
  163.2 0.0 copy-done.1
  163.2 10.1 %convolution_convert_fusion.1 = bf16[512,3072]{1,0:T(8,128)(2,1)} fusion(bf16[512,1536]{1,0:T(8,128)(2,1)S(1)} %copy-done.1, bf16[3072,1536]{1,0:T(8,128)(2,1)} %all-gather.4.cloned.1.call-done), kind=kOutput, calls=%fused_computation.2 | convolution fusion | flops 4833411072 | bytes 14155776 | tf_op jit(solution)/shard_map/dot_general | solution.py:182
  173.3 0.0 reduce-scatter.5.cloned.1.call-update
  173.4 90.1 %reduce-scatter.7.cloned.1.call-done = bf16[384,1536]{1,0:T(8,128)(2,1)} async-done(((bf16[3072,1536]{1,0:T(8,128)(2,1)}), bf16[384,1536]{1,0:T(8,128)(2,1)}) %reduce-scatter.7.cloned.1.call-update) | async-done | bytes 1179664
  263.4 1.7 copy.21
  265.1 1.8 copy.19
  266.9 45.1 %reduce-scatter.5.cloned.1.call-done = bf16[128,3072]{1,0:T(8,128)(2,1)} async-done(((bf16[512,3072]{1,0:T(8,128)(2,1)}), bf16[128,3072]{1,0:T(8,128)(2,1)}) %reduce-scatter.5.cloned.1.call-update) | async-done | bytes 786448 | tf_op jit(solution)/shard_map/reduce_scatter | solution.py:181
  (9 shorter events, 0.1 us)
Async XLA Ops:
  7.2 66.4 %all-gather.6.cloned.1.call-start = ((), (), s32[]{:S(2)}) async-start(), calls=%async_computation.5 | async-start | bytes 3932160 | tf_op jit(solution)/shard_map/all_gather | solution.py:166
  7.9 155.3 %all-gather.4.cloned.1.call-start = ((), (), s32[]{:S(2)}) async-start(), calls=%async_computation.3 | async-start | bytes 10616832 | tf_op jit(solution)/shard_map/all_gather | solution.py:165
  15.7 3.9 %copy-start.2 = (s32[1,2,3]{2,1,0:T(2,128)S(1)}, s32[1,2,3]{2,1,0:T(2,128)}, u32[]{:S(2)}) copy-start(s32[1,2,3]{2,1,0:T(2,128)} %param.10) | copy-start | bytes 76
  15.7 4.2 %copy-start.3 = (s32[1,4,6]{2,1,0:T(4,128)S(1)}, s32[1,4,6]{2,1,0:T(4,128)}, u32[]{:S(2)}) copy-start(s32[1,4,6]{2,1,0:T(4,128)} %param.11) | copy-start | bytes 292
  15.7 37.0 %all-to-all-start = ((bf16[4,128,2048]{2,1,0:T(8,128)(2,1)}), bf16[4,128,2048]{2,1,0:T(8,128)(2,1)S(1)}, u32[]{:S(2)}, u32[]{:S(2)}) async-start(bf16[4,128,2048]{2,1,0:T(8,128)(2,1)} %pad_maximum_fusion), calls=%async_computation | async-start | bytes 4194304 | tf_op jit(solution)/shard_map/all_to_all | solution.py:163
  19.5 2.1 copy-start.4
  19.5 243.9 %reduce-scatter.7.cloned.1.call-start = ((), (), s32[]{:S(2)}) async-start(), calls=%async_computation.6 | async-start | bytes 10616832
  63.7 1.1 copy-start
  96.1 67.1 %copy-start.1 = (bf16[512,1536]{1,0:T(8,128)(2,1)S(1)}, bf16[512,1536]{1,0:T(8,128)(2,1)}, u32[]{:S(2)}) copy-start(bf16[512,1536]{1,0:T(8,128)(2,1)} %copy-done) | copy-start | bytes 4718596
  96.2 215.9 %reduce-scatter.5.cloned.1.call-start = ((), (), s32[]{:S(2)}) async-start(), calls=%async_computation.4 | async-start | bytes 3932160 | tf_op jit(solution)/shard_map/reduce_scatter | solution.py:181
Sparse Core Ops, SparseCore 0:
  9.8 63.6 all-gather.5
  75.2 87.9 all-gather.3
  165.5 97.8 reduce-scatter.6
  266.8 45.1 reduce-scatter.4

commit v2 on v1

--- a/solution.py
+++ b/solution.py
@@ -69,19 +69,23 @@
     return jnp.where(lane < RT, narrow, wide)
 
 
-def attention_kernel(qkv_ref, grad_ref, cos_ref, sin_ref, bias_ref, out_ref, dk_ref, dv_ref):
+def head_backward(qkv_ref, grad_ref, cos_ref, sin_ref, bias_ref, out_ref, dk_ref, dv_ref, head):
     rows = AREA * TILE
     slabs = qkv_ref.shape[0] // rows
     scale = HD ** (-0.5)
     cosine, sine = cos_ref[...], sin_ref[...]
 
+    def lanes(start, count=HD):
+        return pl.ds(pl.multiple_of(start, HD), count)
+
     def rotated(start):
-        values = qkv_ref[:, start : start + HD].astype(jnp.float32)
+        values = qkv_ref[:, lanes(start)].astype(jnp.float32)
         return (values * cosine + partner(values) * sine).astype(jnp.bfloat16)
 
-    rot_q, rot_k = rotated(0), rotated(HD)
-    values = qkv_ref[:, 2 * HD : 3 * HD]
-    grads = grad_ref[...]
+    base = head * (3 * HD)
+    rot_q, rot_k = rotated(base), rotated(base + HD)
+    values = qkv_ref[:, lanes(base + 2 * HD)]
+    grads = grad_ref[:, lanes(head * HD)]
     across = (((1,), (1,)), ((), ()))
     plain = (((1,), (0,)), ((), ()))
     down = (((0,), (0,)), ((), ()))
@@ -111,82 +115,215 @@
         score_grad = (probs * (prob_grad - total) * scale).astype(jnp.bfloat16)
         dq = lax.dot_general(score_grad, key, plain, preferred_element_type=jnp.float32)
         dq = dq * cosine[here] - partner(dq) * sine[here]
-        out_ref[here, 0:HD] = dq.astype(jnp.bfloat16)
+        out_ref[here, lanes(base)] = dq.astype(jnp.bfloat16)
         dk_ref[near, :] += lax.dot_general(
             score_grad, query, down, preferred_element_type=jnp.float32
         )
     dk = dk_ref[...]
-    out_ref[:, HD : 2 * HD] = (dk * cosine - partner(dk) * sine).astype(jnp.bfloat16)
-    out_ref[:, 2 * HD : 3 * HD] = dv_ref[...].astype(jnp.bfloat16)
-
-
-def attention(mixed, cosine, sine, bias):
-    tokens = mixed.shape[0]
-    heads = mixed.shape[1] // (4 * HD)
-    whole = lambda array: pl.BlockSpec(array.shape, lambda head: (0, 0))
+    out_ref[:, lanes(base + HD)] = (dk * cosine - partner(dk) * sine).astype(jnp.bfloat16)
+    out_ref[:, lanes(base + 2 * HD)] = dv_ref[...].astype(jnp.bfloat16)
+
+
+def greet(axis, others):
+    barrier = pltpu.get_barrier_semaphore()
+    for other in others:
+        pl.semaphore_signal(
+            barrier, inc=1, device_id={axis: other}, device_id_type=pl.DeviceIdType.MESH
+        )
+    pl.semaphore_wait(barrier, len(others))
+
+
+def attention_kernel(
+    size, inputs_ref, saved_ref, gout_ref, cos_ref, sin_ref, bias_ref, out_ref, rows_ref,
+    qkv_ref, grad_ref, dk_ref, dv_ref, send_sems, recv_sems, own_sems, send_rows, recv_rows,
+):
+    me = lax.axis_index("seq")
+    tokens, columns = saved_ref.shape
+    heads = columns // size // (3 * HD)
+    others = [lax.rem(me + step, size) for step in range(1, size)]
+    greet("seq", others)
+    mine = pl.ds(pl.multiple_of(me * tokens, TILE), tokens)
+    parts = ((saved_ref, qkv_ref, 3 * HD), (gout_ref, grad_ref, HD))
+
+    def remote(source, target, send, recv, other):
+        return pltpu.make_async_remote_copy(
+            src_ref=source, dst_ref=target, send_sem=send, recv_sem=recv,
+            device_id={"seq": other}, device_id_type=pl.DeviceIdType.MESH,
+        )
+
+    def piece(head, step, at):
+        source, target, width = parts[at]
+        other = others[step]
+        there = pl.ds(pl.multiple_of((other * heads + head) * width, HD), width)
+        here = pl.ds(pl.multiple_of(head * width, HD), width)
+        return remote(
+            source.at[:, there], target.at[mine, here],
+            send_sems.at[head, step, at], recv_sems.at[head, step, at], other,
+        )
+
+    def own(head, at):
+        source, target, width = parts[at]
+        there = pl.ds(pl.multiple_of((me * heads + head) * width, HD), width)
+        here = pl.ds(pl.multiple_of(head * width, HD), width)
+        return pltpu.make_async_copy(
+            source.at[:, there], target.at[mine, here], own_sems.at[head, at]
+        )
+
+    own_rows = pltpu.make_async_copy(inputs_ref, rows_ref.at[mine], own_sems.at[heads, 0])
+    all_rows = [
+        remote(inputs_ref, rows_ref.at[mine], send_rows.at[step], recv_rows.at[step], others[step])
+        for step in range(size - 1)
+    ]
+
+    def launch(head, carry):
+        for at in range(2):
+            own(head, at).start()
+        for step in range(size - 1):
+            for at in range(2):
+                piece(head, step, at).start()
+        return carry
+
+    lax.fori_loop(0, heads, launch, 0)
+    for copy in all_rows:
+        copy.start()
+    own_rows.start()
+
+    def work(head, carry):
+        for at in range(2):
+            own(head, at).wait()
+        for step in range(size - 1):
+            for at in range(2):
+                piece(head, step, at).wait()
+        head_backward(
+            qkv_ref, grad_ref, cos_ref, sin_ref, bias_ref, out_ref, dk_ref, dv_ref, head
+        )
+        return carry
+
+    lax.fori_loop(0, heads, work, 0)
+    own_rows.wait()
+    for copy in all_rows:
+        copy.wait()
+
+
+def attention(size, inputs, saved, gout, cosine, sine, bias):
+    tokens = inputs.shape[0] * size
+    heads = gout.shape[1] // size // HD
+    vmem, anywhere = pl.BlockSpec(memory_space=pltpu.VMEM), pl.BlockSpec(memory_space=pl.ANY)
+    dma = pltpu.SemaphoreType.DMA
     return pl.pallas_call(
-        attention_kernel,
-        grid=(heads,),
-        out_shape=jax.ShapeDtypeStruct((tokens, heads * 3 * HD), jnp.bfloat16),
-        in_specs=[
-            pl.BlockSpec((tokens, 3 * HD), lambda head: (0, head)),
-            pl.BlockSpec((tokens, HD), lambda head: (0, 3 * heads + head)),
-            whole(cosine),
-            whole(sine),
-            whole(bias),
-        ],
-        out_specs=pl.BlockSpec((tokens, 3 * HD), lambda head: (0, head)),
+        functools.partial(attention_kernel, size),
+        out_shape=(
+            jax.ShapeDtypeStruct((tokens, heads * 3 * HD), jnp.bfloat16),
+            jax.ShapeDtypeStruct((tokens, inputs.shape[1]), jnp.bfloat16),
+        ),
+        in_specs=[anywhere] * 3 + [vmem] * 3,
+        out_specs=(vmem, anywhere),
         scratch_shapes=[
+            pltpu.VMEM((tokens, heads * 3 * HD), jnp.bfloat16),
+            pltpu.VMEM((tokens, heads * HD), jnp.bfloat16),
             pltpu.VMEM((tokens, HD), jnp.float32),
             pltpu.VMEM((tokens, HD), jnp.float32),
+            dma((heads, size - 1, 2)),
+            dma((heads, size - 1, 2)),
+            dma((heads + 1, 2)),
+            dma((size - 1,)),
+            dma((size - 1,)),
         ],
-        compiler_params=pltpu.CompilerParams(vmem_limit_bytes=48 * 1024 * 1024),
+        compiler_params=pltpu.CompilerParams(
+            collective_id=0, has_side_effects=True, vmem_limit_bytes=48 * 1024 * 1024
+        ),
         cost_estimate=pl.CostEstimate(
             flops=heads * 10 * tokens * min(tokens, 768) * HD,
-            bytes_accessed=16 * heads * tokens * HD,
+            bytes_accessed=100 * 1024 * 1024,
             transcendentals=heads * tokens * min(tokens, 768),
         ),
-    )(mixed, mixed, cosine, sine, bias)
-
-
-def by_device(rows, parts):
-    tokens, columns = rows.shape
-    return rows.reshape(tokens, parts, columns // parts).transpose(1, 0, 2)
-
-
-def body(seq_size, fsdp_size, inputs, w_qkv, saved_qkv, out_grad, clip_grid, tile_pairs):
+    )(inputs, saved, gout, cosine, sine, bias)
+
+
+def input_kernel(size, grad_ref, weight_ref, out_ref, sent, landed, send_sems, recv_sems):
+    me = lax.axis_index("seq")
+    chunks, width = sent.shape[0], sent.shape[2]
+    tokens = out_ref.shape[0]
+    others = [lax.rem(me + step, size) for step in range(1, size)]
+    greet("seq", others)
+
+    def piece(chunk, step):
+        there = pl.ds(pl.multiple_of(others[step] * tokens, TILE), tokens)
+        return pltpu.make_async_remote_copy(
+            src_ref=sent.at[chunk, there], dst_ref=landed.at[chunk, step],
+            send_sem=send_sems.at[chunk, step], recv_sem=recv_sems.at[chunk, step],
+            device_id={"seq": others[step]}, device_id_type=pl.DeviceIdType.MESH,
+        )
+
+    def product(chunk, carry):
+        here = pl.ds(pl.multiple_of(chunk * width, HD), width)
+        sent[chunk] = lax.dot_general(
+            grad_ref[...], weight_ref[here, :], (((1,), (1,)), ((), ())),
+            preferred_element_type=jnp.float32,
+        ).astype(jnp.bfloat16)
+        for step in range(size - 1):
+            piece(chunk, step).start()
+        return carry
+
+    def add(chunk, carry):
+        here = pl.ds(pl.multiple_of(chunk * width, HD), width)
+        mine = pl.ds(pl.multiple_of(me * tokens, TILE), tokens)
+        total = sent[chunk, mine].astype(jnp.float32)
+        for step in range(size - 1):
+            piece(chunk, step).wait()
+            total = total + landed[chunk, step].astype(jnp.float32)
+        out_ref[:, here] = total.astype(jnp.bfloat16)
+        return carry
+
+    lax.fori_loop(0, chunks, product, 0)
+    lax.fori_loop(0, chunks, add, 0)
+
+
+def input_part(size, qkv_grad, weight):
+    tokens, depth = qkv_grad.shape
+    model = weight.shape[0]
+    width = 3 * HD
+    chunks = model // width
+    vmem = pl.BlockSpec(memory_space=pltpu.VMEM)
+    dma = pltpu.SemaphoreType.DMA
+    return pl.pallas_call(
+        functools.partial(input_kernel, size),
+        out_shape=jax.ShapeDtypeStruct((tokens // size, model), jnp.bfloat16),
+        in_specs=[vmem, vmem],
+        out_specs=vmem,
+        scratch_shapes=[
+            pltpu.VMEM((chunks, tokens, width), jnp.bfloat16),
+            pltpu.VMEM((chunks, size - 1, tokens // size, width), jnp.bfloat16),
+            dma((chunks, size - 1)),
+            dma((chunks, size - 1)),
+        ],
+        compiler_params=pltpu.CompilerParams(
+            collective_id=1, has_side_effects=True, vmem_limit_bytes=56 * 1024 * 1024
+        ),
+        cost_estimate=pl.CostEstimate(
+            flops=2 * tokens * depth * model, bytes_accessed=100 * 1024 * 1024, transcendentals=0
+        ),
+    )(qkv_grad, weight)
+
+
+def body(seq_size, inputs, w_qkv, saved_qkv, out_grad, clip_grid, tile_pairs):
     window = tile_pairs[0]
     tile_count = window.shape[0]
-    mixed = jnp.concatenate(
-        [by_device(saved_qkv[0], seq_size), by_device(out_grad[0], seq_size)], axis=2
-    )
-    mixed = lax.all_to_all(mixed, "seq", split_axis=0, concat_axis=0, tiled=True)
-    mixed = mixed.reshape(-1, mixed.shape[2])
     weight_full = lax.all_gather(w_qkv, "fsdp", axis=0, tiled=True)
-    group_rows = lax.all_gather(inputs[0], "seq", axis=0, tiled=True)
     cosine, sine = rope_tables(clip_grid[0], tile_count)
     listed = jnp.any(
         window[:, :, None] == jnp.arange(tile_count, dtype=jnp.int32)[None, None, :], axis=1
     )
     bias = jnp.repeat(jnp.where(listed, 0.0, -1e30).astype(jnp.float32), TILE, axis=1)
-    qkv_grad = attention(mixed, cosine, sine, bias)
-    weight_part = lax.psum_scatter(
-        lax.dot_general(
-            group_rows, qkv_grad, (((0,), (0,)), ((), ())), preferred_element_type=jnp.float32
-        ).astype(jnp.bfloat16),
-        "fsdp",
-        scatter_dimension=0,
-        tiled=True,
-    ).astype(jnp.float32)
-    input_part = lax.psum_scatter(
-        lax.dot_general(
-            qkv_grad, weight_full, (((1,), (1,)), ((), ())), preferred_element_type=jnp.float32
-        ).astype(jnp.bfloat16),
-        "seq",
-        scatter_dimension=0,
-        tiled=True,
-    )
-    return (input_part[None], weight_part)
+    qkv_grad, group_rows = attention(
+        seq_size, inputs[0], saved_qkv[0], out_grad[0], cosine, sine, bias
+    )
+    product = lax.dot_general(
+        group_rows, qkv_grad, (((0,), (0,)), ((), ())), preferred_element_type=jnp.float32
+    ).astype(jnp.bfloat16)
+    weight_part = lax.psum_scatter(product, "fsdp", scatter_dimension=0, tiled=True)
+    input_grad = input_part(seq_size, qkv_grad, weight_full)
+    return (input_grad[None], weight_part.astype(jnp.float32))
 
 
 def solution(mesh):
@@ -199,5 +336,5 @@
         P("fsdp", None, None),
     )
     out_specs = (P("fsdp", "seq", None), P("fsdp", "seq"))
-    local = functools.partial(body, mesh.shape["seq"], mesh.shape["fsdp"])
+    local = functools.partial(body, mesh.shape["seq"])
     return jax.shard_map(local, mesh=mesh, in_specs=in_specs, out_specs=out_specs, check_vma=False)

time: 321 us -> 214 us (0.67)
  the two profiles are of different devices: /device:TPU:8 before, /device:TPU:0 now
where the time goes in v2:
time: 214 us
  Pallas kernels  106 us (50%)
  waiting for transfers between devices  71.7 us (34%)
  between operations  14.2 us (7%)
  matrix products  9.6 us (4%)
  other arithmetic  8.52 us (4%)
  local copies, waits for them, and re-layouts  4.26 us (2%)
    pallas_call x1, Pallas kernels, attention(): pl.pallas_call(functools.partial(attention_kernel, size), out_shape=(jax....  61.9 us
    reduce_scatter x1, waiting for transfers between devices, body(): lax.psum_scatter(product, 'fsdp', scatter_dimension=0, tiled=True)  56.3 us
    pallas_call x1, Pallas kernels, input_part(): pl.pallas_call(functools.partial(input_kernel, size), out_shape=jax.Shape...  44 us
    all_gather x1, waiting for transfers between devices, body(): weight_full = lax.all_gather(w_qkv, 'fsdp', axis=0, tiled=True)  14.7 us
    dot_general x1, matrix products, body(): lax.dot_general(group_rows, qkv_grad, (((0,), (0,)), ((), ())), preferred...  9.6 us
  transfers between devices with their start and end apart: 2, of which 2 were waited for; matrix products, arithmetic and copies ran while one was open for 8% of the time, Pallas kernels for 49%

profile of v2, /device:TPU:0, one launch (start us, length us, event | category | flops | bytes accessed | tf_op | source)
XLA Modules:
  0.0 214.1 jit_solution(7308835390306757186)
XLA Ops:
  7.2 0.0 copy-start.5
  7.2 0.0 copy-start.1
  7.2 0.0 copy-start
  7.2 0.0 copy-start.2
  7.2 0.0 all-gather.2.cloned.1.call-start
  7.3 0.7 all-gather.2.cloned.1.call-update
  7.9 0.0 reduce-scatter.2.cloned.1.call-start
  8.0 1.0 slice_reduce_fusion.1
  9.0 0.1 reduce
  9.2 0.8 fusion
  10.0 0.1 broadcast_bitcast_fusion
  10.1 0.1 select_reduce_fusion
  10.2 0.3 fusion.4
  10.5 0.1 fusion.3
  10.6 0.1 convert_bitcast_fusion.1
  10.7 0.1 convert_bitcast_fusion
  10.8 0.8 broadcast_multiply_fusion.2
  11.6 0.2 broadcast_multiply_fusion
  11.8 2.1 concatenate.3
  13.9 0.0 copy-done.5
  14.0 1.9 sine_multiply_fusion
  15.8 0.0 copy-done.1
  15.8 0.0 copy-done
  15.8 0.0 copy-done.2
  15.8 61.9 %shard_map.77 = (bf16[512,1536]{1,0:T(8,128)(2,1)S(1)}, bf16[512,3072]{1,0:T(8,128)(2,1)}) custom-call(bf16[128,3072]{1,0:T(8,128)(2,1)S(1)} %bitcast.21, bf16[128,6144]{1,0:T(8,128)(2,1)S(1)} %bitcast.20, bf16[128,2048]{1,0:T(8,128)(2,1)S(1)} %bitcast.22, f32[512,128]{1,0:T(8,128)S(1)} %get-tuple-element.15.cos_ref, ...), custom_call_target="tpu_custom_call" | custom-call | flops 1342177280 | bytes 104857600 | tf_op jit(solution)/shard_map/pallas_call | solution.py:213
  77.7 0.0 copy-start.3
  77.7 1.1 copy-done.3
  78.9 9.6 %convolution_convert_fusion = bf16[3072,1536]{1,0:T(8,128)(2,1)} fusion(bf16[512,3072]{1,0:T(8,128)(2,1)} %get-tuple-element.5, bf16[512,1536]{1,0:T(8,128)(2,1)S(1)} %get-tuple-element.4.grad_ref), kind=kOutput, calls=%fused_computation | convolution fusion | flops 4836556800 | bytes 14155776 | tf_op jit(solution)/shard_map/dot_general | solution.py:321
  88.5 0.0 reduce-scatter.2.cloned.1.call-update
  88.5 14.7 %all-gather.2.cloned.1.call-done.weight_ref = bf16[3072,1536]{1,0:T(8,128)(2,1)} async-done(((bf16[384,1536]{1,0:T(8,128)(2,1)}), bf16[3072,1536]{1,0:T(8,128)(2,1)}) %all-gather.2.cloned.1.call-update) | async-done | bytes 9437200 | tf_op jit(solution)/shard_map/all_gather | solution.py:312
  103.1 44.0 %shard_map.78 = bf16[128,3072]{1,0:T(8,128)(2,1)} custom-call(bf16[512,1536]{1,0:T(8,128)(2,1)} %copy-done.3, bf16[3072,1536]{1,0:T(8,128)(2,1)} %all-gather.2.cloned.1.call-done.weight_ref), custom_call_target="tpu_custom_call" | custom-call | flops 4831838208 | bytes 104857600 | tf_op jit(solution)/shard_map/pallas_call | solution.py:289
  147.2 0.0 copy-start.4
  147.2 56.3 %reduce-scatter.2.cloned.1.call-done = bf16[384,1536]{1,0:T(8,128)(2,1)} async-done(((bf16[3072,1536]{1,0:T(8,128)(2,1)}), bf16[384,1536]{1,0:T(8,128)(2,1)}) %reduce-scatter.2.cloned.1.call-update) | async-done | bytes 1179664 | tf_op jit(solution)/shard_map/reduce_scatter | solution.py:324
  203.5 3.0 %convert_element_type.44 = f32[384,1536]{1,0:T(8,128)} convert(bf16[384,1536]{1,0:T(8,128)(2,1)} %reduce-scatter.2.cloned.1.call-done) | non-fusion elementwise | flops 589824 | bytes 3538944 | tf_op jit(solution)/shard_map/convert_element_type | solution.py:326
  206.4 0.0 copy-done.4
  206.4 0.9 copy.12
  (9 shorter events, 0.1 us)
Async XLA Ops:
  7.2 6.8 %copy-start.5 = (f32[128]{0:T(128)S(1)}, f32[128]{0:T(128)}, u32[]{:S(2)}) copy-start(f32[128]{0:T(128)} %constant.86.clone.1) | copy-start | bytes 1540
  7.2 8.6 %copy-start.1 = (bf16[1,128,3072]{2,1,0:T(8,128)(2,1)S(1)}, bf16[1,128,3072]{2,1,0:T(8,128)(2,1)}, u32[]{:S(2)}) copy-start(bf16[1,128,3072]{2,1,0:T(8,128)(2,1)} %param.6) | copy-start | bytes 2359300
  7.2 8.6 %copy-start = (bf16[1,128,6144]{2,1,0:T(8,128)(2,1)S(1)}, bf16[1,128,6144]{2,1,0:T(8,128)(2,1)}, u32[]{:S(2)}) copy-start(bf16[1,128,6144]{2,1,0:T(8,128)(2,1)} %param.8) | copy-start | bytes 4718596
  7.2 8.6 %copy-start.2 = (bf16[1,128,2048]{2,1,0:T(8,128)(2,1)S(1)}, bf16[1,128,2048]{2,1,0:T(8,128)(2,1)}, u32[]{:S(2)}) copy-start(bf16[1,128,2048]{2,1,0:T(8,128)(2,1)} %param.9) | copy-start | bytes 1572868
  7.2 95.9 %all-gather.2.cloned.1.call-start = ((), (), s32[]{:S(2)}) async-start(), calls=%async_computation.1 | async-start | bytes 10616832 | tf_op jit(solution)/shard_map/all_gather | solution.py:312
  7.9 195.5 %reduce-scatter.2.cloned.1.call-start = ((), (), s32[]{:S(2)}) async-start(), calls=%async_computation.2 | async-start | bytes 10616832 | tf_op jit(solution)/shard_map/reduce_scatter | solution.py:324
  77.7 1.1 copy-start.3
  147.2 59.3 %copy-start.4 = (bf16[128,3072]{1,0:T(8,128)(2,1)S(1)}, bf16[128,3072]{1,0:T(8,128)(2,1)}, u32[]{:S(2)}) copy-start(bf16[128,3072]{1,0:T(8,128)(2,1)} %shard_map.78) | copy-start | bytes 2359300
Sparse Core Ops, SparseCore 0:
  9.7 93.4 all-gather.1
  105.4 97.9 reduce-scatter.1

commit v3 on v2

--- a/solution.py
+++ b/solution.py
@@ -240,22 +240,119 @@
     )(inputs, saved, gout, cosine, sine, bias)
 
 
-def input_kernel(size, grad_ref, weight_ref, out_ref, sent, landed, send_sems, recv_sems):
-    me = lax.axis_index("seq")
+CUTS = 4
+
+
+def grads_kernel(
+    size, spread, grad_ref, weight_hbm, product_ref, out_ref, wout_ref,
+    weight_ref, sent, landed, mine, paired, from_left, from_right,
+    send_sems, recv_sems, weight_sem, own_sems, pair_send, pair_recv,
+    left_send, left_recv, right_send, right_recv,
+):
+    me, row = lax.axis_index("seq"), lax.axis_index("fsdp")
+    depth = spread // 2
+    z, core = row // 2, row % 2
     chunks, width = sent.shape[0], sent.shape[2]
     tokens = out_ref.shape[0]
+    height = wout_ref.shape[0]
+    cut = height // CUTS
     others = [lax.rem(me + step, size) for step in range(1, size)]
-    greet("seq", others)
+    pair = row + 1 - 2 * core
+    up, down = lax.rem(row + 2, spread), lax.rem(row + spread - 2, spread)
+
+    barrier = pltpu.get_barrier_semaphore()
+
+    def hail(axis, other):
+        pl.semaphore_signal(
+            barrier, inc=1, device_id={axis: other}, device_id_type=pl.DeviceIdType.MESH
+        )
+
+    for other in others:
+        hail("seq", other)
+    hail("fsdp", pair)
+    hail("fsdp", down)
+    hail("fsdp", up)
+    pl.semaphore_wait(barrier, size + 2)
+
+    load = pltpu.make_async_copy(weight_hbm, weight_ref, weight_sem)
+
+    def rows_of(block, side, at):
+        return pl.ds(pl.multiple_of((block * 2 + side) * height + at * cut, 16), cut)
+
+    def part(at):
+        return pl.ds(pl.multiple_of(at * cut, 16), cut)
+
+    def own(block, at):
+        return pltpu.make_async_copy(
+            product_ref.at[rows_of(block, core, at)], mine.at[block, part(at)],
+            own_sems.at[block, at],
+        )
+
+    def remote(source, target, send, recv, axis, other):
+        return pltpu.make_async_remote_copy(
+            src_ref=source, dst_ref=target, send_sem=send, recv_sem=recv,
+            device_id={axis: other}, device_id_type=pl.DeviceIdType.MESH,
+        )
+
+    def to_pair(block, at):
+        return remote(
+            product_ref.at[rows_of(block, 1 - core, at)], paired.at[block, part(at)],
+            pair_send.at[block, at], pair_recv.at[block, at], "fsdp", pair,
+        )
+
+    def to_up(block, at):
+        return remote(
+            mine.at[block, part(at)], from_left.at[block, part(at)],
+            left_send.at[block, at], left_recv.at[block, at], "fsdp", up,
+        )
+
+    def to_down(block, at):
+        return remote(
+            mine.at[block, part(at)], from_right.at[block, part(at)],
+            right_send.at[block, at], right_recv.at[block, at], "fsdp", down,
+        )
 
     def piece(chunk, step):
         there = pl.ds(pl.multiple_of(others[step] * tokens, TILE), tokens)
-        return pltpu.make_async_remote_copy(
-            src_ref=sent.at[chunk, there], dst_ref=landed.at[chunk, step],
-            send_sem=send_sems.at[chunk, step], recv_sem=recv_sems.at[chunk, step],
-            device_id={"seq": others[step]}, device_id_type=pl.DeviceIdType.MESH,
-        )
-
-    def product(chunk, carry):
+        return remote(
+            sent.at[chunk, there], landed.at[chunk, step],
+            send_sems.at[chunk, step], recv_sems.at[chunk, step], "seq", others[step],
+        )
+
+    def launch(index, carry):
+        turn, at = index // CUTS, index % CUTS
+        half = turn // 2
+        block = half + (1 - turn % 2) * (depth - 1 - 2 * half)
+        to_pair(block, at).start()
+        own(block, at).start()
+        return carry
+
+    lax.fori_loop(0, depth * CUTS, launch, 0)
+    load.start()
+
+    def pair_sum(block, at):
+        own(block, at).wait()
+        to_pair(block, at).wait()
+        return mine[block, part(at), :].astype(jnp.float32) + paired[
+            block, part(at), :
+        ].astype(jnp.float32)
+
+    def forward(block, at, has_behind, copy, behind):
+        total = pair_sum(block, at)
+
+        @pl.when(has_behind)
+        def _():
+            copy(block, at).wait_recv()
+            more = total + behind[block, part(at), :].astype(jnp.float32)
+            mine[block, part(at), :] = more.astype(jnp.bfloat16)
+
+        @pl.when(jnp.logical_not(has_behind))
+        def _():
+            mine[block, part(at), :] = total.astype(jnp.bfloat16)
+
+        copy(block, at).start()
+
+    def product(chunk):
         here = pl.ds(pl.multiple_of(chunk * width, HD), width)
         sent[chunk] = lax.dot_general(
             grad_ref[...], weight_ref[here, :], (((1,), (1,)), ((), ())),
@@ -263,50 +360,118 @@
         ).astype(jnp.bfloat16)
         for step in range(size - 1):
             piece(chunk, step).start()
-        return carry
+
+    steps = (depth - 1) * CUTS
+
+    def advance(index, carry):
+        turn, at = index // CUTS, index % CUTS
+
+        @pl.when(z < depth - 1 - turn)
+        def _():
+            forward(depth - 1 - turn, at, z > 0, to_up, from_left)
+
+        @pl.when(z > turn)
+        def _():
+            forward(turn, at, z < depth - 1, to_down, from_right)
+
+        @pl.when(index == 0)
+        def _():
+            load.wait()
+
+        @pl.when(index < chunks)
+        def _():
+            product(index)
+
+        return carry
+
+    lax.fori_loop(0, steps, advance, 0)
+    for chunk in range(steps, chunks):
+        product(chunk)
 
     def add(chunk, carry):
         here = pl.ds(pl.multiple_of(chunk * width, HD), width)
-        mine = pl.ds(pl.multiple_of(me * tokens, TILE), tokens)
-        total = sent[chunk, mine].astype(jnp.float32)
+        own_rows = pl.ds(pl.multiple_of(me * tokens, TILE), tokens)
+        total = sent[chunk, own_rows].astype(jnp.float32)
         for step in range(size - 1):
             piece(chunk, step).wait()
             total = total + landed[chunk, step].astype(jnp.float32)
         out_ref[:, here] = total.astype(jnp.bfloat16)
         return carry
 
-    lax.fori_loop(0, chunks, product, 0)
     lax.fori_loop(0, chunks, add, 0)
 
-
-def input_part(size, qkv_grad, weight):
-    tokens, depth = qkv_grad.shape
+    def finish(at, carry):
+        wout_ref[part(at), :] = pair_sum(z, at)
+
+        @pl.when(z > 0)
+        def _():
+            to_up(z, at).wait_recv()
+            wout_ref[part(at), :] += from_left[z, part(at), :].astype(jnp.float32)
+
+        @pl.when(z < depth - 1)
+        def _():
+            to_down(z, at).wait_recv()
+            wout_ref[part(at), :] += from_right[z, part(at), :].astype(jnp.float32)
+
+        return carry
+
+    lax.fori_loop(0, CUTS, finish, 0)
+
+    def settle(index, carry):
+        turn, at = index // CUTS, index % CUTS
+
+        @pl.when(z < depth - 1 - turn)
+        def _():
+            to_up(depth - 1 - turn, at).wait_send()
+
+        @pl.when(z > turn)
+        def _():
+            to_down(turn, at).wait_send()
+
+        return carry
+
+    lax.fori_loop(0, steps, settle, 0)
+
+
+def both_grads(size, spread, qkv_grad, weight, product):
+    tokens, columns = qkv_grad.shape
     model = weight.shape[0]
     width = 3 * HD
     chunks = model // width
-    vmem = pl.BlockSpec(memory_space=pltpu.VMEM)
+    depth, height = spread // 2, model // spread
+    vmem, anywhere = pl.BlockSpec(memory_space=pltpu.VMEM), pl.BlockSpec(memory_space=pl.ANY)
     dma = pltpu.SemaphoreType.DMA
+    blocks = pltpu.VMEM((depth, height, columns), jnp.bfloat16)
     return pl.pallas_call(
-        functools.partial(input_kernel, size),
-        out_shape=jax.ShapeDtypeStruct((tokens // size, model), jnp.bfloat16),
-        in_specs=[vmem, vmem],
-        out_specs=vmem,
+        functools.partial(grads_kernel, size, spread),
+        out_shape=(
+            jax.ShapeDtypeStruct((tokens // size, model), jnp.bfloat16),
+            jax.ShapeDtypeStruct((height, columns), jnp.float32),
+        ),
+        in_specs=[vmem, anywhere, anywhere],
+        out_specs=(vmem, vmem),
         scratch_shapes=[
+            pltpu.VMEM((model, columns), jnp.bfloat16),
             pltpu.VMEM((chunks, tokens, width), jnp.bfloat16),
             pltpu.VMEM((chunks, size - 1, tokens // size, width), jnp.bfloat16),
+            blocks, blocks, blocks, blocks,
             dma((chunks, size - 1)),
             dma((chunks, size - 1)),
-        ],
+            dma,
+        ]
+        + [dma((depth, CUTS))] * 7,
         compiler_params=pltpu.CompilerParams(
-            collective_id=1, has_side_effects=True, vmem_limit_bytes=56 * 1024 * 1024
+            collective_id=1, has_side_effects=True, vmem_limit_bytes=58 * 1024 * 1024
         ),
         cost_estimate=pl.CostEstimate(
-            flops=2 * tokens * depth * model, bytes_accessed=100 * 1024 * 1024, transcendentals=0
+            flops=2 * tokens * columns * model,
+            bytes_accessed=200 * 1024 * 1024,
+            transcendentals=0,
         ),
-    )(qkv_grad, weight)
-
-
-def body(seq_size, inputs, w_qkv, saved_qkv, out_grad, clip_grid, tile_pairs):
+    )(qkv_grad, weight, product)
+
+
+def body(seq_size, fsdp_size, inputs, w_qkv, saved_qkv, out_grad, clip_grid, tile_pairs):
     window = tile_pairs[0]
     tile_count = window.shape[0]
     weight_full = lax.all_gather(w_qkv, "fsdp", axis=0, tiled=True)
@@ -321,9 +486,8 @@
     product = lax.dot_general(
         group_rows, qkv_grad, (((0,), (0,)), ((), ())), preferred_element_type=jnp.float32
     ).astype(jnp.bfloat16)
-    weight_part = lax.psum_scatter(product, "fsdp", scatter_dimension=0, tiled=True)
-    input_grad = input_part(seq_size, qkv_grad, weight_full)
-    return (input_grad[None], weight_part.astype(jnp.float32))
+    input_grad, weight_grad = both_grads(seq_size, fsdp_size, qkv_grad, weight_full, product)
+    return (input_grad[None], weight_grad)
 
 
 def solution(mesh):
@@ -336,5 +500,5 @@
         P("fsdp", None, None),
     )
     out_specs = (P("fsdp", "seq", None), P("fsdp", "seq"))
-    local = functools.partial(body, mesh.shape["seq"])
+    local = functools.partial(body, mesh.shape["seq"], mesh.shape["fsdp"])
     return jax.shard_map(local, mesh=mesh, in_specs=in_specs, out_specs=out_specs, check_vma=False)

time: 214 us -> 209 us (0.977)
  the two profiles are of different devices: /device:TPU:0 before, /device:TPU:8 now
where the time goes in v3:
time: 209 us; the launch traced here: 208 us
  Pallas kernels  158 us (76%)
  waiting for transfers between devices  14.3 us (7%)
  between operations  14.2 us (7%)
  matrix products  10.2 us (5%)
  local copies, waits for them, and re-layouts  7.98 us (4%)
  other arithmetic  3.91 us (2%)
    pallas_call x1, Pallas kernels, both_grads(): pl.pallas_call(functools.partial(grads_kernel, size, spread), out_shape=(...  97.5 us
    pallas_call x1, Pallas kernels, attention(): pl.pallas_call(functools.partial(attention_kernel, size), out_shape=(jax....  60.4 us
    all_gather x1, waiting for transfers between devices, body(): weight_full = lax.all_gather(w_qkv, 'fsdp', axis=0, tiled=True)  13.7 us
    dot_general x1, matrix products, body(): lax.dot_general(group_rows, qkv_grad, (((0,), (0,)), ((), ())), preferred...  10.2 us
    unnamed x14, local copies, waits for them, and re-layouts  7.55 us
  transfers between devices with their start and end apart: 1, of which 1 were waited for; matrix products, arithmetic and copies ran while one was open for 7% of the time, Pallas kernels for 29%

profile of v3, /device:TPU:8, one launch (start us, length us, event | category | flops | bytes accessed | tf_op | source)
XLA Modules:
  0.0 208.5 jit_solution(12974327253297913175)
XLA Ops:
  7.2 0.0 copy-start.4
  7.2 0.0 copy-start.1
  7.2 0.0 all-gather.2.cloned.1.call-start
  7.2 0.7 all-gather.2.cloned.1.call-update
  7.9 1.0 slice_reduce_fusion.1
  9.0 0.1 reduce
  9.1 0.8 fusion
  9.9 0.1 broadcast_bitcast_fusion
  10.1 0.1 select_reduce_fusion
  10.2 0.3 fusion.4
  10.4 0.1 fusion.3
  10.6 0.1 convert_bitcast_fusion.1
  10.6 0.1 convert_bitcast_fusion
  10.7 0.1 broadcast_multiply_fusion.2
  10.8 0.2 broadcast_multiply_fusion
  11.0 0.4 concatenate.3
  11.5 0.0 copy-done.4
  11.5 0.9 sine_multiply_fusion
  12.4 0.0 copy-done.1
  12.4 0.0 copy-start.2
  12.4 1.1 copy-done.2
  13.6 0.0 copy-start.3
  13.6 1.0 copy-done.3
  14.6 60.4 %shard_map.77 = (bf16[512,1536]{1,0:T(8,128)(2,1)S(1)}, bf16[512,3072]{1,0:T(8,128)(2,1)}) custom-call(bf16[128,3072]{1,0:T(8,128)(2,1)S(1)} %bitcast.21, bf16[128,6144]{1,0:T(8,128)(2,1)S(1)} %bitcast.20, bf16[128,2048]{1,0:T(8,128)(2,1)S(1)} %bitcast.22, f32[512,128]{1,0:T(8,128)S(1)} %get-tuple-element.19.cos_ref, ...), custom_call_target="tpu_custom_call" | custom-call | flops 1342177280 | bytes 104857600 | tf_op jit(solution)/shard_map/pallas_call | solution.py:213
  75.0 0.0 copy-start
  75.0 10.2 %convolution_convert_fusion.product_ref = bf16[3072,1536]{1,0:T(8,128)(2,1)} fusion(bf16[512,3072]{1,0:T(8,128)(2,1)} %get-tuple-element.7, bf16[512,1536]{1,0:T(8,128)(2,1)S(1)} %get-tuple-element.6.grad_ref), kind=kOutput, calls=%fused_computation | convolution fusion | flops 4836556800 | bytes 14155776 | tf_op jit(solution)/shard_map/dot_general | solution.py:486
  85.2 0.0 copy-done
  85.2 13.7 %all-gather.2.cloned.1.call-done.weight_hbm = bf16[3072,1536]{1,0:T(8,128)(2,1)} async-done(((bf16[384,1536]{1,0:T(8,128)(2,1)}), bf16[3072,1536]{1,0:T(8,128)(2,1)}) %all-gather.2.cloned.1.call-update) | async-done | bytes 9437200 | tf_op jit(solution)/shard_map/all_gather | solution.py:477
  98.8 97.5 %shard_map.78 = (bf16[128,3072]{1,0:T(8,128)(2,1)}, f32[384,1536]{1,0:T(8,128)}) custom-call(bf16[512,1536]{1,0:T(8,128)(2,1)} %copy-done, bf16[3072,1536]{1,0:T(8,128)(2,1)} %all-gather.2.cloned.1.call-done.weight_hbm, bf16[3072,1536]{1,0:T(8,128)(2,1)} %convolution_convert_fusion.product_ref), custom_call_target="tpu_custom_call" | custom-call | flops 4831838208 | bytes 209715200 | tf_op jit(solution)/shard_map/pallas_call | solution.py:445
  196.4 2.1 copy.13
  198.4 3.2 %copy.14 = f32[384,1536]{1,0:T(8,128)} copy(f32[384,1536]{1,0:T(8,128)} %get-tuple-element.29) | data formatting | bytes 4718592
  (9 shorter events, 0.1 us)
Async XLA Ops:
  7.2 4.3 %copy-start.4 = (f32[128]{0:T(128)S(1)}, f32[128]{0:T(128)}, u32[]{:S(2)}) copy-start(f32[128]{0:T(128)} %constant.86.clone.1) | copy-start | bytes 1540
  7.2 5.2 %copy-start.1 = (bf16[1,128,6144]{2,1,0:T(8,128)(2,1)S(1)}, bf16[1,128,6144]{2,1,0:T(8,128)(2,1)}, u32[]{:S(2)}) copy-start(bf16[1,128,6144]{2,1,0:T(8,128)(2,1)} %param.8) | copy-start | bytes 4718596
  7.2 91.6 %all-gather.2.cloned.1.call-start = ((), (), s32[]{:S(2)}) async-start(), calls=%async_computation | async-start | bytes 10616832 | tf_op jit(solution)/shard_map/all_gather | solution.py:477
  12.4 1.1 copy-start.2
  13.6 1.0 copy-start.3
  75.0 10.2 %copy-start = (bf16[512,1536]{1,0:T(8,128)(2,1)}, bf16[512,1536]{1,0:T(8,128)(2,1)S(1)}, u32[]{:S(2)}) copy-start(bf16[512,1536]{1,0:T(8,128)(2,1)S(1)} %get-tuple-element.6.grad_ref) | copy-start | bytes 4718596
Sparse Core Ops, SparseCore 0:
  9.7 89.1 all-gather.1

commit v4 on v3

--- a/solution.py
+++ b/solution.py
@@ -240,24 +240,85 @@
     )(inputs, saved, gout, cosine, sine, bias)
 
 
-CUTS = 4
+CUTS = 6
+
+
+def pair_kernel(product_ref, out_ref, landed, own_sems, send_sems, recv_sems):
+    row = lax.axis_index("fsdp")
+    core = row % 2
+    pair = row + 1 - 2 * core
+    depth, height = out_ref.shape[0], out_ref.shape[1]
+    barrier = pltpu.get_barrier_semaphore()
+    pl.semaphore_signal(
+        barrier, inc=1, device_id={"fsdp": pair}, device_id_type=pl.DeviceIdType.MESH
+    )
+    pl.semaphore_wait(barrier, 1)
+
+    def rows_of(block, side):
+        return pl.ds(pl.multiple_of((block * 2 + side) * height, 16), height)
+
+    def own(block):
+        return pltpu.make_async_copy(
+            product_ref.at[rows_of(block, core)], out_ref.at[block], own_sems.at[block]
+        )
+
+    def across(block):
+        return pltpu.make_async_remote_copy(
+            src_ref=product_ref.at[rows_of(block, 1 - core)], dst_ref=landed.at[block],
+            send_sem=send_sems.at[block], recv_sem=recv_sems.at[block],
+            device_id={"fsdp": pair}, device_id_type=pl.DeviceIdType.MESH,
+        )
+
+    def launch(block, carry):
+        across(block).start()
+        own(block).start()
+        return carry
+
+    def add(block, carry):
+        own(block).wait()
+        across(block).wait()
+        total = out_ref[block].astype(jnp.float32) + landed[block].astype(jnp.float32)
+        out_ref[block] = total.astype(jnp.bfloat16)
+        return carry
+
+    lax.fori_loop(0, depth, launch, 0)
+    lax.fori_loop(0, depth, add, 0)
+
+
+def pair_sums(spread, product):
+    model, columns = product.shape
+    depth, height = spread // 2, model // spread
+    dma = pltpu.SemaphoreType.DMA
+    return pl.pallas_call(
+        pair_kernel,
+        out_shape=jax.ShapeDtypeStruct((depth, height, columns), jnp.bfloat16),
+        in_specs=[pl.BlockSpec(memory_space=pl.ANY)],
+        out_specs=pl.BlockSpec(memory_space=pltpu.VMEM),
+        scratch_shapes=[pltpu.VMEM((depth, height, columns), jnp.bfloat16)]
+        + [dma((depth,))] * 3,
+        compiler_params=pltpu.CompilerParams(
+            collective_id=2, has_side_effects=True, vmem_limit_bytes=32 * 1024 * 1024
+        ),
+        cost_estimate=pl.CostEstimate(
+            flops=model * columns, bytes_accessed=8 * model * columns, transcendentals=0
+        ),
+    )(product)
 
 
 def grads_kernel(
     size, spread, grad_ref, weight_hbm, product_ref, out_ref, wout_ref,
-    weight_ref, sent, landed, mine, paired, from_left, from_right,
-    send_sems, recv_sems, weight_sem, own_sems, pair_send, pair_recv,
+    weight_ref, sent, landed, mine, from_left, from_right,
+    send_sems, recv_sems, weight_sem, own_sems,
     left_send, left_recv, right_send, right_recv,
 ):
     me, row = lax.axis_index("seq"), lax.axis_index("fsdp")
     depth = spread // 2
-    z, core = row // 2, row % 2
+    z = row // 2
     chunks, width = sent.shape[0], sent.shape[2]
     tokens = out_ref.shape[0]
     height = wout_ref.shape[0]
     cut = height // CUTS
     others = [lax.rem(me + step, size) for step in range(1, size)]
-    pair = row + 1 - 2 * core
     up, down = lax.rem(row + 2, spread), lax.rem(row + spread - 2, spread)
 
     barrier = pltpu.get_barrier_semaphore()
@@ -269,22 +330,18 @@
 
     for other in others:
         hail("seq", other)
-    hail("fsdp", pair)
     hail("fsdp", down)
     hail("fsdp", up)
-    pl.semaphore_wait(barrier, size + 2)
+    pl.semaphore_wait(barrier, size + 1)
 
     load = pltpu.make_async_copy(weight_hbm, weight_ref, weight_sem)
-
-    def rows_of(block, side, at):
-        return pl.ds(pl.multiple_of((block * 2 + side) * height + at * cut, 16), cut)
 
     def part(at):
         return pl.ds(pl.multiple_of(at * cut, 16), cut)
 
     def own(block, at):
         return pltpu.make_async_copy(
-            product_ref.at[rows_of(block, core, at)], mine.at[block, part(at)],
+            product_ref.at[block, part(at)], mine.at[block, part(at)],
             own_sems.at[block, at],
         )
 
@@ -292,12 +349,6 @@
         return pltpu.make_async_remote_copy(
             src_ref=source, dst_ref=target, send_sem=send, recv_sem=recv,
             device_id={axis: other}, device_id_type=pl.DeviceIdType.MESH,
-        )
-
-    def to_pair(block, at):
-        return remote(
-            product_ref.at[rows_of(block, 1 - core, at)], paired.at[block, part(at)],
-            pair_send.at[block, at], pair_recv.at[block, at], "fsdp", pair,
         )
 
     def to_up(block, at):
@@ -323,22 +374,18 @@
         turn, at = index // CUTS, index % CUTS
         half = turn // 2
         block = half + (1 - turn % 2) * (depth - 1 - 2 * half)
-        to_pair(block, at).start()
         own(block, at).start()
         return carry
 
     lax.fori_loop(0, depth * CUTS, launch, 0)
     load.start()
 
-    def pair_sum(block, at):
+    def own_part(block, at):
         own(block, at).wait()
-        to_pair(block, at).wait()
-        return mine[block, part(at), :].astype(jnp.float32) + paired[
-            block, part(at), :
-        ].astype(jnp.float32)
+        return mine[block, part(at), :].astype(jnp.float32)
 
     def forward(block, at, has_behind, copy, behind):
-        total = pair_sum(block, at)
+        total = own_part(block, at)
 
         @pl.when(has_behind)
         def _():
@@ -401,7 +448,7 @@
     lax.fori_loop(0, chunks, add, 0)
 
     def finish(at, carry):
-        wout_ref[part(at), :] = pair_sum(z, at)
+        wout_ref[part(at), :] = own_part(z, at)
 
         @pl.when(z > 0)
         def _():
@@ -454,12 +501,12 @@
             pltpu.VMEM((model, columns), jnp.bfloat16),
             pltpu.VMEM((chunks, tokens, width), jnp.bfloat16),
             pltpu.VMEM((chunks, size - 1, tokens // size, width), jnp.bfloat16),
-            blocks, blocks, blocks, blocks,
+            blocks, blocks, blocks,
             dma((chunks, size - 1)),
             dma((chunks, size - 1)),
             dma,
         ]
-        + [dma((depth, CUTS))] * 7,
+        + [dma((depth, CUTS))] * 5,
         compiler_params=pltpu.CompilerParams(
             collective_id=1, has_side_effects=True, vmem_limit_bytes=58 * 1024 * 1024
         ),
@@ -486,7 +533,8 @@
     product = lax.dot_general(
         group_rows, qkv_grad, (((0,), (0,)), ((), ())), preferred_element_type=jnp.float32
     ).astype(jnp.bfloat16)
-    input_grad, weight_grad = both_grads(seq_size, fsdp_size, qkv_grad, weight_full, product)
+    summed = pair_sums(fsdp_size, product)
+    input_grad, weight_grad = both_grads(seq_size, fsdp_size, qkv_grad, weight_full, summed)
     return (input_grad[None], weight_grad)
 
 

time: 209 us -> 212 us (1.014)
  Pallas kernels: 158 us -> 169 us
  waiting for transfers between devices: 14.3 us -> 4.62 us
  matrix products: 10.2 us -> 7.86 us
    all_gather x1, waiting for transfers between devices: 13.7 us -> 3.94 us  [body(): weight_full = lax.all_gather(w_qkv, 'fsdp', axis=0, tiled=True)]
    pallas_call x0 -> x1, Pallas kernels: none -> 8.53 us  [pair_sums(): pl.pallas_call(pair_kernel, out_shape=jax.ShapeDtypeStruct((depth, height...]
    pallas_call x1, Pallas kernels: 97.5 us -> 100 us  [both_grads(): pl.pallas_call(functools.partial(grads_kernel, size, spread), out_shape=(...]
    dot_general x1, matrix products: 10.2 us -> 7.86 us  [body(): lax.dot_general(group_rows, qkv_grad, (((0,), (0,)), ((), ())), preferred...]
    unnamed x14 -> x16, local copies, waits for them, and re-layouts: 7.55 us -> 7.62 us
  transfers between devices with their start and end apart: 1 -> 1, of which waited for: 1 -> 1; matrix products, arithmetic and copies ran while one was open for 7% -> 7% of each run, Pallas kernels for 29% -> 33%
where the time goes in v4:
time: 212 us; the launch traced here: 211 us
  Pallas kernels  169 us (80%)
  between operations  14.2 us (7%)
  local copies, waits for them, and re-layouts  9.76 us (5%)
  matrix products  7.86 us (4%)
  other arithmetic  5.58 us (3%)
  waiting for transfers between devices  4.62 us (2%)
    pallas_call x1, Pallas kernels, both_grads(): pl.pallas_call(functools.partial(grads_kernel, size, spread), out_shape=(...  100 us
    pallas_call x1, Pallas kernels, attention(): pl.pallas_call(functools.partial(attention_kernel, size), out_shape=(jax....  60.4 us
    pallas_call x1, Pallas kernels, pair_sums(): pl.pallas_call(pair_kernel, out_shape=jax.ShapeDtypeStruct((depth, height...  8.53 us
    dot_general x1, matrix products, body(): lax.dot_general(group_rows, qkv_grad, (((0,), (0,)), ((), ())), preferred...  7.86 us
    unnamed x16, local copies, waits for them, and re-layouts  7.62 us
  transfers between devices with their start and end apart: 1, of which 1 were waited for; matrix products, arithmetic and copies ran while one was open for 7% of the time, Pallas kernels for 33%

profile of v4, /device:TPU:8, one launch (start us, length us, event | category | flops | bytes accessed | tf_op | source)
XLA Modules:
  0.0 211.0 jit_solution(8516047261677108727)
XLA Ops:
  7.2 0.0 copy-start.5
  7.2 0.0 copy-start.2
  7.2 0.0 copy-start.1
  7.2 0.0 copy-start.3
  7.2 0.0 all-gather.2.cloned.1.call-start
  7.3 0.7 all-gather.2.cloned.1.call-update
  7.9 1.0 slice_reduce_fusion.1
  9.0 0.1 reduce
  9.1 0.8 fusion
  10.0 0.1 broadcast_bitcast_fusion
  10.1 0.1 select_reduce_fusion
  10.2 0.3 fusion.4
  10.5 0.1 fusion.3
  10.6 0.1 convert_bitcast_fusion.1
  10.7 0.1 convert_bitcast_fusion
  10.7 0.8 broadcast_multiply_fusion.2
  11.6 0.2 broadcast_multiply_fusion
  11.8 2.1 %concatenate.3 = f32[512,128]{1,0:T(8,128)} concatenate(f32[512,8]{1,0:T(8,128)} %broadcast_multiply_fusion.2, f32[512,8]{1,0:T(8,128)} %broadcast_multiply_fusion.2, f32[512,28]{1,0:T(8,128)S(1)} %get-tuple-element.23, f32[512,28]{1,0:T(8,128)S(1)} %get-tuple-element.23, f32[512,28]{1,0:T(8,128)S(1)} %get-tuple-element.22, f32[512,28]{1,0:T(8,128)S(1)} %get-tuple-element.22), dimensions={1} | concatenate | bytes 524288 | tf_op jit(solution)/shard_map/concatenate | solution.py:52
  13.9 0.0 copy-done.5
  13.9 1.9 sine_multiply_fusion
  15.8 0.0 copy-done.2
  15.8 0.0 copy-done.1
  15.8 0.0 copy-done.3
  15.8 60.4 %shard_map.77 = (bf16[512,1536]{1,0:T(8,128)(2,1)S(1)}, bf16[512,3072]{1,0:T(8,128)(2,1)}) custom-call(bf16[128,3072]{1,0:T(8,128)(2,1)S(1)} %bitcast.21, bf16[128,6144]{1,0:T(8,128)(2,1)S(1)} %bitcast.20, bf16[128,2048]{1,0:T(8,128)(2,1)S(1)} %bitcast.22, f32[512,128]{1,0:T(8,128)S(1)} %get-tuple-element.19.cos_ref, ...), custom_call_target="tpu_custom_call" | custom-call | flops 1342177280 | bytes 104857600 | tf_op jit(solution)/shard_map/pallas_call | solution.py:213
  76.2 0.0 copy-start.4
  76.3 7.9 %convolution_convert_fusion.product_ref = bf16[3072,1536]{1,0:T(8,128)(2,1)S(1)} fusion(bf16[512,3072]{1,0:T(8,128)(2,1)} %get-tuple-element.7, bf16[512,1536]{1,0:T(8,128)(2,1)S(1)} %get-tuple-element.6.grad_ref), kind=kOutput, calls=%fused_computation | convolution fusion | flops 4836556800 | bytes 14155776 | tf_op jit(solution)/shard_map/dot_general | solution.py:533
  84.1 0.0 copy-done.4
  84.1 8.5 %shard_map.78.product_ref = bf16[4,384,1536]{2,1,0:T(8,128)(2,1)S(1)} custom-call(bf16[3072,1536]{1,0:T(8,128)(2,1)S(1)} %convolution_convert_fusion.product_ref), custom_call_target="tpu_custom_call" | custom-call | flops 4718592 | bytes 37748736 | tf_op jit(solution)/shard_map/pallas_call | solution.py:292
  92.7 0.0 copy-start
  92.7 2.2 %copy-done = bf16[4,384,1536]{2,1,0:T(8,128)(2,1)} copy-done((bf16[4,384,1536]{2,1,0:T(8,128)(2,1)}, bf16[4,384,1536]{2,1,0:T(8,128)(2,1)S(1)}, u32[]{:S(2)}) %copy-start) | copy-done | bytes 4718616
  94.9 3.9 %all-gather.2.cloned.1.call-done.weight_hbm = bf16[3072,1536]{1,0:T(8,128)(2,1)} async-done(((bf16[384,1536]{1,0:T(8,128)(2,1)}), bf16[3072,1536]{1,0:T(8,128)(2,1)}) %all-gather.2.cloned.1.call-update) | async-done | bytes 9437200 | tf_op jit(solution)/shard_map/all_gather | solution.py:524
  98.8 100.0 %shard_map.79 = (bf16[128,3072]{1,0:T(8,128)(2,1)}, f32[384,1536]{1,0:T(8,128)}) custom-call(bf16[512,1536]{1,0:T(8,128)(2,1)} %copy-done.4, bf16[3072,1536]{1,0:T(8,128)(2,1)} %all-gather.2.cloned.1.call-done.weight_hbm, bf16[4,384,1536]{2,1,0:T(8,128)(2,1)} %copy-done), custom_call_target="tpu_custom_call" | custom-call | flops 4831838208 | bytes 209715200 | tf_op jit(solution)/shard_map/pallas_call | solution.py:492
  198.9 2.1 copy.13
  200.9 3.2 %copy.14 = f32[384,1536]{1,0:T(8,128)} copy(f32[384,1536]{1,0:T(8,128)} %get-tuple-element.29) | data formatting | bytes 4718592
  (9 shorter events, 0.1 us)
Async XLA Ops:
  7.2 6.8 %copy-start.5 = (f32[128]{0:T(128)S(1)}, f32[128]{0:T(128)}, u32[]{:S(2)}) copy-start(f32[128]{0:T(128)} %constant.86.clone.1) | copy-start | bytes 1540
  7.2 8.6 %copy-start.2 = (bf16[1,128,3072]{2,1,0:T(8,128)(2,1)S(1)}, bf16[1,128,3072]{2,1,0:T(8,128)(2,1)}, u32[]{:S(2)}) copy-start(bf16[1,128,3072]{2,1,0:T(8,128)(2,1)} %param.6) | copy-start | bytes 2359300
  7.2 8.6 %copy-start.1 = (bf16[1,128,6144]{2,1,0:T(8,128)(2,1)S(1)}, bf16[1,128,6144]{2,1,0:T(8,128)(2,1)}, u32[]{:S(2)}) copy-start(bf16[1,128,6144]{2,1,0:T(8,128)(2,1)} %param.8) | copy-start | bytes 4718596
  7.2 8.6 %copy-start.3 = (bf16[1,128,2048]{2,1,0:T(8,128)(2,1)S(1)}, bf16[1,128,2048]{2,1,0:T(8,128)(2,1)}, u32[]{:S(2)}) copy-start(bf16[1,128,2048]{2,1,0:T(8,128)(2,1)} %param.9) | copy-start | bytes 1572868
  7.2 91.6 %all-gather.2.cloned.1.call-start = ((), (), s32[]{:S(2)}) async-start(), calls=%async_computation | async-start | bytes 10616832 | tf_op jit(solution)/shard_map/all_gather | solution.py:524
  76.2 7.9 %copy-start.4 = (bf16[512,1536]{1,0:T(8,128)(2,1)}, bf16[512,1536]{1,0:T(8,128)(2,1)S(1)}, u32[]{:S(2)}) copy-start(bf16[512,1536]{1,0:T(8,128)(2,1)S(1)} %get-tuple-element.6.grad_ref) | copy-start | bytes 4718596
  92.7 2.2 %copy-start = (bf16[4,384,1536]{2,1,0:T(8,128)(2,1)}, bf16[4,384,1536]{2,1,0:T(8,128)(2,1)S(1)}, u32[]{:S(2)}) copy-start(bf16[4,384,1536]{2,1,0:T(8,128)(2,1)S(1)} %shard_map.78.product_ref) | copy-start | bytes 14155780
Sparse Core Ops, SparseCore 0:
  9.7 89.1 all-gather.1

commit v5 on v3

--- a/solution.py
+++ b/solution.py
@@ -240,7 +240,7 @@
     )(inputs, saved, gout, cosine, sine, bias)
 
 
-CUTS = 4
+CUTS = 3
 
 
 def grads_kernel(

time: 209 us -> 212 us (1.014)
  Pallas kernels: 158 us -> 161 us
    pallas_call x1, Pallas kernels: 97.5 us -> 100 us  [both_grads(): pl.pallas_call(functools.partial(grads_kernel, size, spread), out_shape=(...]
where the time goes in v5:
time: 212 us; the launch traced here: 211 us
  Pallas kernels  161 us (76%)
  waiting for transfers between devices  14.3 us (7%)
  between operations  14.2 us (7%)
  matrix products  10.2 us (5%)
  local copies, waits for them, and re-layouts  7.98 us (4%)
  other arithmetic  3.91 us (2%)
    pallas_call x1, Pallas kernels, both_grads(): pl.pallas_call(functools.partial(grads_kernel, size, spread), out_shape=(...  100 us
    pallas_call x1, Pallas kernels, attention(): pl.pallas_call(functools.partial(attention_kernel, size), out_shape=(jax....  60.4 us
    all_gather x1, waiting for transfers between devices, body(): weight_full = lax.all_gather(w_qkv, 'fsdp', axis=0, tiled=True)  13.7 us
    dot_general x1, matrix products, body(): lax.dot_general(group_rows, qkv_grad, (((0,), (0,)), ((), ())), preferred...  10.2 us
    unnamed x14, local copies, waits for them, and re-layouts  7.55 us
  transfers between devices with their start and end apart: 1, of which 1 were waited for; matrix products, arithmetic and copies ran while one was open for 7% of the time, Pallas kernels for 29%

profile of v5, /device:TPU:8, one launch (start us, length us, event | category | flops | bytes accessed | tf_op | source)
XLA Modules:
  0.0 211.1 jit_solution(11194099625522858389)
XLA Ops:
  7.2 0.0 copy-start.4
  7.2 0.0 copy-start.1
  7.2 0.0 all-gather.2.cloned.1.call-start
  7.2 0.7 all-gather.2.cloned.1.call-update
  7.9 1.0 slice_reduce_fusion.1
  9.0 0.1 reduce
  9.1 0.8 fusion
  9.9 0.1 broadcast_bitcast_fusion
  10.1 0.1 select_reduce_fusion
  10.2 0.3 fusion.4
  10.4 0.1 fusion.3
  10.6 0.1 convert_bitcast_fusion.1
  10.6 0.1 convert_bitcast_fusion
  10.7 0.1 broadcast_multiply_fusion.2
  10.8 0.2 broadcast_multiply_fusion
  11.0 0.4 concatenate.3
  11.5 0.0 copy-done.4
  11.5 0.9 sine_multiply_fusion
  12.4 0.0 copy-done.1
  12.4 0.0 copy-start.2
  12.4 1.1 copy-done.2
  13.6 0.0 copy-start.3
  13.6 1.0 copy-done.3
  14.6 60.4 %shard_map.77 = (bf16[512,1536]{1,0:T(8,128)(2,1)S(1)}, bf16[512,3072]{1,0:T(8,128)(2,1)}) custom-call(bf16[128,3072]{1,0:T(8,128)(2,1)S(1)} %bitcast.21, bf16[128,6144]{1,0:T(8,128)(2,1)S(1)} %bitcast.20, bf16[128,2048]{1,0:T(8,128)(2,1)S(1)} %bitcast.22, f32[512,128]{1,0:T(8,128)S(1)} %get-tuple-element.19.cos_ref, ...), custom_call_target="tpu_custom_call" | custom-call | flops 1342177280 | bytes 104857600 | tf_op jit(solution)/shard_map/pallas_call | solution.py:213
  75.0 0.0 copy-start
  75.0 10.2 %convolution_convert_fusion.product_ref = bf16[3072,1536]{1,0:T(8,128)(2,1)} fusion(bf16[512,3072]{1,0:T(8,128)(2,1)} %get-tuple-element.7, bf16[512,1536]{1,0:T(8,128)(2,1)S(1)} %get-tuple-element.6.grad_ref), kind=kOutput, calls=%fused_computation | convolution fusion | flops 4836556800 | bytes 14155776 | tf_op jit(solution)/shard_map/dot_general | solution.py:486
  85.2 0.0 copy-done
  85.2 13.7 %all-gather.2.cloned.1.call-done.weight_hbm = bf16[3072,1536]{1,0:T(8,128)(2,1)} async-done(((bf16[384,1536]{1,0:T(8,128)(2,1)}), bf16[3072,1536]{1,0:T(8,128)(2,1)}) %all-gather.2.cloned.1.call-update) | async-done | bytes 9437200 | tf_op jit(solution)/shard_map/all_gather | solution.py:477
  98.8 100.2 %shard_map.78 = (bf16[128,3072]{1,0:T(8,128)(2,1)}, f32[384,1536]{1,0:T(8,128)}) custom-call(bf16[512,1536]{1,0:T(8,128)(2,1)} %copy-done, bf16[3072,1536]{1,0:T(8,128)(2,1)} %all-gather.2.cloned.1.call-done.weight_hbm, bf16[3072,1536]{1,0:T(8,128)(2,1)} %convolution_convert_fusion.product_ref), custom_call_target="tpu_custom_call" | custom-call | flops 4831838208 | bytes 209715200 | tf_op jit(solution)/shard_map/pallas_call | solution.py:445
  199.0 2.1 copy.13
  201.1 3.2 %copy.14 = f32[384,1536]{1,0:T(8,128)} copy(f32[384,1536]{1,0:T(8,128)} %get-tuple-element.29) | data formatting | bytes 4718592
  (9 shorter events, 0.1 us)
Async XLA Ops:
  7.2 4.3 %copy-start.4 = (f32[128]{0:T(128)S(1)}, f32[128]{0:T(128)}, u32[]{:S(2)}) copy-start(f32[128]{0:T(128)} %constant.86.clone.1) | copy-start | bytes 1540
  7.2 5.2 %copy-start.1 = (bf16[1,128,6144]{2,1,0:T(8,128)(2,1)S(1)}, bf16[1,128,6144]{2,1,0:T(8,128)(2,1)}, u32[]{:S(2)}) copy-start(bf16[1,128,6144]{2,1,0:T(8,128)(2,1)} %param.8) | copy-start | bytes 4718596
  7.2 91.6 %all-gather.2.cloned.1.call-start = ((), (), s32[]{:S(2)}) async-start(), calls=%async_computation | async-start | bytes 10616832 | tf_op jit(solution)/shard_map/all_gather | solution.py:477
  12.4 1.1 copy-start.2
  13.6 1.0 copy-start.3
  75.0 10.2 %copy-start = (bf16[512,1536]{1,0:T(8,128)(2,1)}, bf16[512,1536]{1,0:T(8,128)(2,1)S(1)}, u32[]{:S(2)}) copy-start(bf16[512,1536]{1,0:T(8,128)(2,1)S(1)} %get-tuple-element.6.grad_ref) | copy-start | bytes 4718596
Sparse Core Ops, SparseCore 0:
  9.7 89.1 all-gather.1
